TPU v7x, 128 devices: a whole 4x4x4 slice. The times are simulated.
128 devices in a mesh: dp: 16 (over x, z_lo, core), ctx: 8 (over y, z_hi).
Axes of the slice: x: 4, y: 4, z: 4 (z_hi: 2, z_lo: 2; z = z_hi * 2 + z_lo), core: 2. Of those that a mesh axis runs over, the one named last changes fastest.
Arguments:
- hidden: bfloat16 [16, 1024, 5120], P('dp', 'ctx'), may hold values from -6 to 6
- queries: bfloat16 [16, 1024, 8192], P('dp', 'ctx'), may hold values from -6 to 6
- attn_keys: bfloat16 [16, 1024, 1024], P('dp', 'ctx'), may hold values from -6 to 6
- attn_values: bfloat16 [16, 1024, 1024], P('dp', 'ctx'), may hold values from -6 to 6
- attn_output: bfloat16 [16, 1024, 8192], P('dp', 'ctx'), may hold values from -6 to 6
- output_grad: bfloat16 [16, 1024, 8192], P('dp', 'ctx'), may hold values from -6 to 6
- softmax_lse: float32 [16, 64, 1024], P('dp', None, 'ctx'), may hold values from 4 to 7
- doc_lengths: int32 [16, 8], P('dp'), may hold values from 1 to 512, 1024 in all within a row
- stretch_order: int32 [16, 16], P('dp'), may hold values from 0 to 15, each once within a row
Outputs:
- query_grad: bfloat16 [16, 1024, 8192], P('dp', 'ctx')
- key_grad: bfloat16 [16, 1024, 1024], P('dp', 'ctx')
- value_grad: bfloat16 [16, 1024, 1024], P('dp', 'ctx')
- value_weight_grad: float32 [5120, 1024], P(('dp', 'ctx'))
Inputs may be any that keep to these rules, and one draw needn't show every extreme that they name: `doc_lengths`: each row holds the lengths of the 8 documents of one sequence in order of position; they sum to 1024 and the longest is exactly 512. Each row names every block of 64 positions of its sequence once: stored block j holds positions stretch_order[b, j] * 64 to stretch_order[b, j] * 64 + 63.
All inputs are finite; a program needn't handle non-finite values.
Results may differ from a plain program's by a relative error of at most 0.0052.
Values may be sent and summed in bfloat16 or wider, within the bound.
A program may use at most 128 MiB of HBM per device.

v0:
```python
import math

import jax
import jax.numpy as jnp
from jax import lax
from jax.sharding import PartitionSpec as P

QH = 64
KVH = 8
HD = 128


def stored_positions(first_row, row_count, block_len, block_order):
    row_ids = first_row + jnp.arange(row_count, dtype=jnp.int32)
    slot_ids = row_ids // block_len
    matches = slot_ids[:, None] == jnp.arange(block_order.shape[0], dtype=jnp.int32)[None, :]
    block_ids = jnp.sum(jnp.where(matches, block_order[None, :], 0), axis=1)
    return block_ids * block_len + row_ids % block_len


def document_ids(positions, doc_ends):
    return jnp.sum((positions[:, None] >= doc_ends[None, :]).astype(jnp.int32), axis=1)


def body(
    hidden,
    queries,
    attn_keys,
    attn_values,
    attn_output,
    output_grad,
    softmax_lse,
    doc_lengths,
    stretch_order,
):
    ctx_count = lax.axis_size("ctx")
    ctx_rank = lax.axis_index("ctx")
    shard_len = queries.shape[1]
    block_len = shard_len // 2
    seq_len = shard_len * ctx_count
    head_groups = QH // KVH
    softmax_scale = HD ** (-0.5)
    block_order = stretch_order[0]
    doc_ends = jnp.cumsum(doc_lengths[0], dtype=jnp.int32)
    query_pos = stored_positions(ctx_rank * shard_len, shard_len, block_len, block_order)
    query_doc = document_ids(query_pos, doc_ends)
    query_rows = queries[0].reshape(shard_len, KVH, head_groups, HD)
    grad_rows = output_grad[0].reshape(shard_len, KVH, head_groups, HD)
    out_rows = attn_output[0].reshape(shard_len, KVH, head_groups, HD)
    delta_rows = jnp.sum(grad_rows.astype(jnp.float32) * out_rows.astype(jnp.float32), axis=3)
    delta_rows = jnp.transpose(delta_rows, (1, 2, 0))[..., None]
    lse_rows = softmax_lse[0].reshape(KVH, head_groups, shard_len, 1)
    initial = (
        jnp.zeros((shard_len, KVH, head_groups, HD), jnp.float32),
        jnp.zeros((seq_len, 2 * KVH * HD), jnp.float32),
    )
    key_piece = lax.all_gather(attn_keys[0], "ctx", axis=0, tiled=True)
    value_piece = lax.all_gather(attn_values[0], "ctx", axis=0, tiled=True)
    piece_len = key_piece.shape[0]
    block_width = math.gcd(piece_len, 256)

    def one_block(block_index, state):
        offset = block_index * block_width
        key_block = lax.dynamic_slice_in_dim(key_piece, offset, block_width, 0).reshape(
            block_width, KVH, HD
        )
        value_block = lax.dynamic_slice_in_dim(value_piece, offset, block_width, 0).reshape(
            block_width, KVH, HD
        )
        key_pos = stored_positions(offset, block_width, block_len, block_order)
        key_doc = document_ids(key_pos, doc_ends)
        allowed = (query_pos[:, None] >= key_pos[None, :]) & (
            query_doc[:, None] == key_doc[None, :]
        )
        query_acc, partial_rows = state
        scores = (
            jnp.einsum("tcgd,ncd->cgtn", query_rows, key_block, preferred_element_type=jnp.float32)
            * softmax_scale
        )
        probs = jnp.where(allowed, jnp.exp(scores - lse_rows), 0.0)
        value_part = jnp.einsum(
            "cgtn,tcgd->ncd",
            probs.astype(jnp.bfloat16),
            grad_rows,
            preferred_element_type=jnp.float32,
        )
        prob_grad = jnp.einsum(
            "tcgd,ncd->cgtn", grad_rows, value_block, preferred_element_type=jnp.float32
        )
        score_grad = (probs * (prob_grad - delta_rows) * softmax_scale).astype(jnp.bfloat16)
        query_acc = query_acc + jnp.einsum(
            "cgtn,ncd->tcgd", score_grad, key_block, preferred_element_type=jnp.float32
        )
        key_part = jnp.einsum(
            "cgtn,tcgd->ncd", score_grad, query_rows, preferred_element_type=jnp.float32
        )
        new_rows = jnp.concatenate(
            [key_part.reshape(block_width, KVH * HD), value_part.reshape(block_width, KVH * HD)],
            axis=1,
        )
        current = lax.dynamic_slice_in_dim(partial_rows, offset, block_width, 0)
        partial_rows = lax.dynamic_update_slice_in_dim(partial_rows, current + new_rows, offset, 0)
        return (query_acc, partial_rows)

    query_acc, partial_rows = lax.fori_loop(0, piece_len // block_width, one_block, initial)
    own_rows = lax.psum_scatter(partial_rows, "ctx", scatter_dimension=0, tiled=True)
    query_grad = query_acc.reshape(shard_len, QH * HD).astype(jnp.bfloat16)
    key_grad = own_rows[:, : KVH * HD].astype(jnp.bfloat16)
    value_grad = own_rows[:, KVH * HD :].astype(jnp.bfloat16)
    hidden_rows = hidden[0]
    weight_grad = lax.psum_scatter(
        lax.dot_general(
            hidden_rows, value_grad, (((0,), (0,)), ((), ())), preferred_element_type=jnp.float32
        ),
        ("dp", "ctx"),
        scatter_dimension=0,
        tiled=True,
    )
    return (query_grad[None], key_grad[None], value_grad[None], weight_grad)


def solution(mesh):
    placed = (
        P("dp", "ctx", None),
        P("dp", "ctx", None),
        P("dp", "ctx", None),
        P("dp", "ctx", None),
        P("dp", "ctx", None),
        P("dp", "ctx", None),
        P("dp", None, "ctx"),
        P("dp", None),
        P("dp", None),
    )
    return jax.shard_map(
        body,
        mesh=mesh,
        in_specs=placed,
        out_specs=(
            P("dp", "ctx", None),
            P("dp", "ctx", None),
            P("dp", "ctx", None),
            P(("dp", "ctx"), None),
        ),
        check_vma=False,
    )
```

profile of v0, /device:TPU:0, one launch (start us, length us, event | category | flops | bytes accessed | tf_op | source)
XLA Modules:
  0.0 1098.5 jit_solution(4105105124657520788)
XLA Ops:
  11.9 3.2 copy.63
  15.1 4.1 copy.65
  19.2 4.3 copy.66
  23.7 3.7 multiply_reduce_fusion
  27.4 43.5 %all-gather.5.cloned.1.call-done = bf16[1,1024,1024]{1,2,0:T(8,128)(2,1)} async-done(((bf16[1,128,1024]{1,2,0:T(8,128)(2,1)}), bf16[1,1024,1024]{1,2,0:T(8,128)(2,1)}) %all-gather.5.cloned.1.call-update) | async-done | bytes 2097168 | tf_op jit(solution)/shard_map/all_gather | solution.py:57
  70.9 59.1 %all-gather.7.cloned.1.call-done = bf16[1,1024,1024]{1,2,0:T(8,128)(2,1)} async-done(((bf16[1,128,1024]{1,2,0:T(8,128)(2,1)}), bf16[1,1024,1024]{1,2,0:T(8,128)(2,1)}) %all-gather.7.cloned.1.call-update) | async-done | bytes 2097168 | tf_op jit(solution)/shard_map/all_gather | solution.py:58
  130.0 4.3 broadcast_in_dim.118.clone
  134.2 117.7 %while.18 = (s32[]{:T(128)}, f32[128,8,8,128]{0,3,2,1:T(8,128)}, f32[1024,2048]{1,0:T(8,128)}, bf16[1024,1024]{0,1:T(8,128)(2,1)}, s32[128]{0:T(128)S(1)}, /*ind...) while((s32[]{:T(128)}, f32[128,8,8,128]{0,3,2,1:T(8,128)}, ...), condition=%wide.region_7.8_spmd.clone, body=%wide.region_4.7_spmd.clone.sunk | while | flops 2710692864 | bytes 138095120 | solution.py:105
  136.8 3.1 constant_dynamic-slice_fusion.6
  140.0 2.9 copy.93
  147.1 3.2 fusion.57
  157.6 2.9 copy.94
  160.5 3.2 constant_dynamic-update-slice_fusion.2
  166.3 3.1 constant_dynamic-slice_fusion.6
  169.4 2.9 copy.93
  176.5 3.2 fusion.57
  187.1 2.9 copy.94
  190.0 3.1 constant_dynamic-update-slice_fusion.2
  195.7 3.1 constant_dynamic-slice_fusion.6
  198.8 2.9 copy.93
  206.0 3.2 fusion.57
  216.5 2.9 copy.94
  219.4 3.1 constant_dynamic-update-slice_fusion.2
  225.1 3.1 constant_dynamic-slice_fusion.6
  228.3 2.9 copy.93
  235.4 3.2 fusion.57
  245.9 2.9 copy.94
  248.8 3.2 constant_dynamic-update-slice_fusion.2
  252.2 113.0 %reduce-scatter.5.cloned.1.call-done = f32[128,2048]{1,0:T(8,128)} async-done(((f32[1024,2048]{1,0:T(8,128)}), f32[128,2048]{1,0:T(8,128)}) %reduce-scatter.5.cloned.1.call-update) | async-done | bytes 1048592 | tf_op jit(solution)/shard_map/reduce_scatter | solution.py:106
  366.5 8.6 convolution_bitcast_fusion
  375.1 21.3 %copy.85 = f32[5120,1024]{1,0:T(8,128)} copy(f32[5120,1024]{0,1:T(8,128)} %convolution_bitcast_fusion) | data formatting | bytes 41943040
  403.8 688.2 %reduce-scatter.7.cloned.1.call-done = f32[40,1024]{1,0:T(8,128)} async-done(((f32[5120,1024]{1,0:T(8,128)}), f32[40,1024]{1,0:T(8,128)}) %reduce-scatter.7.cloned.1.call-update) | async-done | bytes 163856
  (120 shorter events, 70.1 us)
Async XLA Ops:
  7.2 359.3 %copy-start = (bf16[1,128,5120]{2,1,0:T(8,128)(2,1)S(1)}, bf16[1,128,5120]{2,1,0:T(8,128)(2,1)}, u32[]{:S(2)}) copy-start(bf16[1,128,5120]{2,1,0:T(8,128)(2,1)} %param.11) | copy-start | bytes 3932164
  7.2 63.7 %all-gather.5.cloned.1.call-start = ((), (), s32[]{:S(2)}) async-start(), calls=%async_computation.3 | async-start | bytes 2359296 | tf_op jit(solution)/shard_map/all_gather | solution.py:57
  9.1 120.8 %all-gather.7.cloned.1.call-start = ((), (), s32[]{:S(2)}) async-start(), calls=%async_computation.4 | async-start | bytes 2359296 | tf_op jit(solution)/shard_map/all_gather | solution.py:58
  11.0 354.2 %reduce-scatter.5.cloned.1.call-start = ((), (), s32[]{:S(2)}) async-start(), calls=%async_computation.2 | async-start | bytes 9437184 | tf_op jit(solution)/shard_map/reduce_scatter | solution.py:106
  19.2 4.3 copy-start.8
  130.0 4.3 copy-start.9
  142.9 2.5 copy-start.6
  145.4 1.7 copy-start.5
  150.3 2.2 copy-start.2
  150.3 2.3 copy-start.4
  152.6 3.5 copy-start.1
  154.1 1.9 copy-start.3
  172.3 2.5 copy-start.6
  174.8 1.7 copy-start.5
  179.7 2.2 copy-start.2
  179.7 2.3 copy-start.4
  182.0 3.5 copy-start.1
  183.6 1.9 copy-start.3
  201.7 2.5 copy-start.6
  204.2 1.7 copy-start.5
  209.1 2.2 copy-start.2
  209.1 2.3 copy-start.4
  211.4 3.5 copy-start.1
  213.0 1.9 copy-start.3
  231.2 2.5 copy-start.6
  233.6 1.7 copy-start.5
  238.5 2.2 copy-start.2
  238.6 2.3 copy-start.4
  240.8 3.5 copy-start.1
  242.4 1.9 copy-start.3
  252.0 840.0 %reduce-scatter.7.cloned.1.call-start = ((), (), s32[]{:S(2)}) async-start(), calls=%async_computation.5 | async-start | bytes 21135360
  366.5 8.6 copy-start.7
Sparse Core Ops, SparseCore 0:
  10.8 60.0 all-gather.4
  73.7 56.2 all-gather.6
  252.1 113.0 reduce-scatter.4
  396.6 695.3 reduce-scatter.6
where the time goes:
time: 1100 us
  waiting for transfers between devices  904 us (82%)
  local copies, waits for them, and re-layouts  114 us (10%)
  matrix products  50 us (5%)
  other arithmetic  16.3 us (1%)
  between operations  13.8 us (1%)
    unnamed x5, waiting for transfers between devices  688 us
    reduce_scatter x1, waiting for transfers between devices, body(): lax.psum_scatter(partial_rows, 'ctx', scatter_dimension=0, tiled=True)  113 us
    all_gather x1, waiting for transfers between devices, body(): value_piece = lax.all_gather(attn_values[0], 'ctx', axis=0, tiled=True)  59.1 us
    all_gather x1, waiting for transfers between devices, body(): key_piece = lax.all_gather(attn_keys[0], 'ctx', axis=0, tiled=True)  43.5 us
    unnamed x13, local copies, waits for them, and re-layouts  32.3 us
    dynamic_update_slice x8, local copies, waits for them, and re-layouts, one_block(): lax.dynamic_update_slice_in_dim(partial_rows, current + new_rows, offset, 0)  24.2 us
    dynamic_slice x8, local copies, waits for them, and re-layouts, one_block(): current = lax.dynamic_slice_in_dim(partial_rows, offset, block_width, 0)  24.1 us
  transfers between devices with their start and end apart: 4, of which 4 were waited for; matrix products, arithmetic and copies ran while one was open for 2% of the time, Pallas kernels for 0%

commit v1 on v0

v1 whole, which is shorter than its diff:
```python
import functools
import math

import jax
import jax.numpy as jnp
from jax import lax
from jax.experimental import pallas as pl
from jax.experimental.pallas import tpu as pltpu
from jax.sharding import PartitionSpec as P

MESH = pl.DeviceIdType.MESH
F32 = jnp.float32
BF16 = jnp.bfloat16
KVH = 8
GRP = 8
HD = 128
ROWS = 128
SEQ = 1024
SCALE = HD ** (-0.5)
LOG2E = math.log2(math.e)
BIG = 3.0e38
NB = 256

A0, A1P, A1M, A3P, A3M, B1P, B1M, B2P, B2M, B3 = range(10)


def dot(a, b, ca, cb):
    return lax.dot_general(a, b, (((ca,), (cb,)), ((), ())), preferred_element_type=F32)


def attention_kernel(
    doc_ref, ord_ref, q_ref, k_ref, v_ref, o_ref, do_ref, lse_ref,
    dq_ref, dk_ref, dv_ref,
    kvb, qb, dob, ob, cap, lser, deltar, pf, dqt, dqs,
    s1, r1, s2, r2, s3, r3, fin,
    send, recv, lsem, dqsem,
):
    ctx = lax.axis_index("ctx")
    y, zh = ctx // 2, lax.rem(ctx, 2)
    partner = y * 2 + 1 - zh
    yp, ym, yo = lax.rem(y + 1, 4), lax.rem(y + 3, 4), lax.rem(y + 2, 4)
    up, down = yp * 2 + zh, ym * 2 + zh

    def load_kv(g):
        cols = pl.ds(pl.multiple_of(g * HD, HD), HD)
        rows = pl.ds(pl.multiple_of(ctx * ROWS, ROWS), ROWS)
        pltpu.make_async_copy(k_ref.at[0, :, cols], kvb.at[g, 0, rows], lsem.at[0]).start()
        pltpu.make_async_copy(v_ref.at[0, :, cols], kvb.at[g, 1, rows], lsem.at[0]).start()

    lax.fori_loop(0, KVH, lambda g, c: (load_kv(g), c)[1], 0)

    def load_heads(h, c):
        cols = pl.ds(pl.multiple_of(h * HD, HD), HD)
        g = h // GRP
        rows = pl.ds(pl.multiple_of(lax.rem(h, GRP) * ROWS, ROWS), ROWS)
        pltpu.make_async_copy(do_ref.at[0, :, cols], dob.at[g, rows], lsem.at[1]).start()
        pltpu.make_async_copy(o_ref.at[0, :, cols], ob.at[g, rows], lsem.at[2]).start()
        pltpu.make_async_copy(q_ref.at[0, :, cols], qb.at[g, rows], lsem.at[3]).start()
        return c

    lax.fori_loop(0, KVH * GRP, load_heads, 0)

    barrier = pltpu.get_barrier_semaphore()
    for c in (partner, up, down):
        pl.semaphore_signal(barrier, inc=1, device_id={"ctx": c}, device_id_type=MESH)
    own = pl.ds(pl.multiple_of(ctx * ROWS, ROWS), ROWS)
    pltpu.make_async_copy(kvb.at[:, :, own], kvb.at[:, :, own], lsem.at[0]).wait()
    pl.semaphore_wait(barrier, 3)

    def slot(s):
        return pl.ds(pl.multiple_of(s * 2 * ROWS, 2 * ROWS), 2 * ROWS)

    def half(s, z):
        return pl.ds(pl.multiple_of(s * 2 * ROWS + z * ROWS, ROWS), ROWS)

    def msg(kind, g):
        if kind == A0:
            ref, dst, to = kvb.at[g, :, own], kvb.at[g, :, own], partner
        elif kind == A1P:
            ref, dst, to = kvb.at[g, :, slot(y)], kvb.at[g, :, slot(y)], up
        elif kind == A1M:
            ref, dst, to = kvb.at[g, :, slot(y)], kvb.at[g, :, slot(y)], down
        elif kind == A3P:
            ref, dst, to = kvb.at[g, :, half(ym, 0)], kvb.at[g, :, half(ym, 0)], up
        elif kind == A3M:
            ref, dst, to = kvb.at[g, :, half(yp, 1)], kvb.at[g, :, half(yp, 1)], down
        elif kind == B1P:
            ref, dst, to = s1.at[g, 0], r1.at[g, 0], up
        elif kind == B1M:
            ref, dst, to = s1.at[g, 1], r1.at[g, 1], down
        elif kind == B2P:
            ref, dst, to = s2.at[g, 0], r2.at[g, 0], up
        elif kind == B2M:
            ref, dst, to = s2.at[g, 1], r2.at[g, 1], down
        else:
            ref, dst, to = s3.at[g], r3.at[g], partner
        return pltpu.make_async_remote_copy(
            src_ref=ref, dst_ref=dst, send_sem=send.at[kind, g], recv_sem=recv.at[kind, g],
            device_id={"ctx": to}, device_id_type=MESH,
        )

    def start_a0(g, c):
        msg(A0, g).start()
        return c

    lax.fori_loop(0, KVH, start_a0, 0)

    lane = lax.broadcasted_iota(jnp.int32, (1, ROWS), 1)
    pos_q = jnp.where(
        lane < 64, ord_ref[0, 2 * ctx] * 64 + lane, ord_ref[0, 2 * ctx + 1] * 64 + lane - 64
    )
    start_q = jnp.zeros((1, ROWS), jnp.int32)
    end = jnp.int32(0)
    for j in range(8):
        end = end + doc_ref[0, j]
        start_q = jnp.where(pos_q >= end, end, start_q)
    for j in range(16):
        pos_n = ord_ref[0, j] * 64 + lax.broadcasted_iota(jnp.int32, (64, ROWS), 0)
        seen = (pos_n <= pos_q) & (pos_n >= start_q)
        cap[j * 64:(j + 1) * 64, :] = jnp.where(seen, BIG, -BIG)

    def a1(g):
        msg(A0, g).wait_recv()
        msg(A1P, g).start()
        msg(A1M, g).start()

    def a3(g):
        msg(A1P, g).wait_recv()
        msg(A3P, g).start()
        msg(A1M, g).wait_recv()
        msg(A3M, g).start()

    a1(0)
    a1(1)
    for n in (1, 2, 3):
        ref = (dob, ob, qb)[n - 1]
        pltpu.make_async_copy(ref, ref, lsem.at[n]).wait()

    def rows_of(g, c):
        heads = lse_ref[0, pl.ds(pl.multiple_of(g * GRP, GRP), GRP), :] * LOG2E
        for h in range(GRP):
            cols = slice(h * ROWS, (h + 1) * ROWS)
            prod = dob[g, cols, :].astype(F32) * ob[g, cols, :].astype(F32)
            deltar[g, :, cols] = jnp.sum(prod.T, axis=0, keepdims=True)
            lser[g, :, cols] = heads[h:h + 1, :]
        return c

    lax.fori_loop(0, KVH, rows_of, 0)
    a3(0)

    def compute(g):
        dqt[...] = jnp.zeros_like(dqt)

        def keys(nb, c):
            r = pl.ds(pl.multiple_of(nb * NB, NB), NB)
            kk, vv = kvb[g, 0, r, :], kvb[g, 1, r, :]
            top = cap[r, :]
            top = jnp.concatenate([top, top], axis=1)
            dk = dv = None
            for hp in range(4):
                cols = slice(hp * 256, (hp + 1) * 256)
                qq, dd = qb[g, cols, :], dob[g, cols, :]
                st = dot(kk, qq, 1, 1)
                p = jnp.exp2(jnp.minimum(st * (SCALE * LOG2E) - lser[g, :, cols], top))
                dp = dot(vv, dd, 1, 1)
                ds = (p * (dp - deltar[g, :, cols]) * SCALE).astype(BF16)
                pv, pk = dot(p.astype(BF16), dd, 1, 0), dot(ds, qq, 1, 0)
                dv, dk = (pv, pk) if dv is None else (dv + pv, dk + pk)
                dqt[:, cols] += dot(kk, ds, 0, 0)
            pf[g, 0, r, :] = dk
            pf[g, 1, r, :] = dv
            return c

        lax.fori_loop(0, SEQ // NB, keys, 0)
        for h in range(GRP):
            cols = slice(h * ROWS, (h + 1) * ROWS)
            dqs[g, :, cols] = dqt[:, cols].T.astype(BF16)
        dq_copy(g).start()

    def dq_copy(g):
        cols = pl.ds(pl.multiple_of(g * GRP * HD, GRP * HD), GRP * HD)
        return pltpu.make_async_copy(dqs.at[g], dq_ref.at[0, :, cols], dqsem.at[g])

    def b1(g):
        s1[g, 0] = pf[g, :, half(yo, 0), :].astype(BF16)
        msg(B1P, g).start()
        s1[g, 1] = pf[g, :, half(yo, 1), :].astype(BF16)
        msg(B1M, g).start()

    def b2(g):
        s2[g, 0, :, ROWS:, :] = pf[g, :, half(yp, 1), :].astype(BF16)
        s2[g, 1, :, :ROWS, :] = pf[g, :, half(ym, 0), :].astype(BF16)
        msg(B1P, g).wait_recv()
        s2[g, 0, :, :ROWS, :] = (pf[g, :, half(yp, 0), :] + r1[g, 0].astype(F32)).astype(BF16)
        msg(B2P, g).start()
        msg(B1M, g).wait_recv()
        s2[g, 1, :, ROWS:, :] = (pf[g, :, half(ym, 1), :] + r1[g, 1].astype(F32)).astype(BF16)
        msg(B2M, g).start()

    def b3(g):
        msg(B2P, g).wait_recv()
        msg(B2M, g).wait_recv()

        def total(z):
            rows = pl.ds(pl.multiple_of(z * ROWS, ROWS), ROWS)
            return (
                pf[g, :, half(y, z), :] + r2[g, 0, :, rows, :].astype(F32) + r2[g, 1, :, rows, :].astype(F32)
            )

        s3[g] = total(1 - zh)
        msg(B3, g).start()
        fin[g] = total(zh)

    def b4(g):
        msg(B3, g).wait_recv()
        cols = pl.ds(pl.multiple_of(g * HD, HD), HD)
        done = (fin[g] + r3[g]).astype(BF16)
        dk_ref[0, :, cols] = done[0]
        dv_ref[0, :, cols] = done[1]

    def step(i, c):
        @pl.when(i + 2 < KVH)
        def _():
            a1(i + 2)

        @pl.when(i + 1 < KVH)
        def _():
            a3(i + 1)

        @pl.when(i < KVH)
        def _():
            msg(A3P, i).wait_recv()
            msg(A3M, i).wait_recv()
            compute(i)
            b1(i)

        @pl.when((i >= 1) & (i - 1 < KVH))
        def _():
            b2(i - 1)

        @pl.when((i >= 2) & (i - 2 < KVH))
        def _():
            b3(i - 2)

        @pl.when(i >= 3)
        def _():
            b4(i - 3)

        return c

    lax.fori_loop(0, KVH + 3, step, 0)

    def finish(g, c):
        for kind in range(10):
            msg(kind, g).wait_send()
        dq_copy(g).wait()
        return c

    lax.fori_loop(0, KVH, finish, 0)


def weight_kernel(
    h_ref, vg_ref, out_ref, hid, ht, hg, vgb, dws, dwr, lsem, hs, hr, vs, vr, ws, wr
):
    dp, ctx = lax.axis_index("dp"), lax.axis_index("ctx")
    x, zl, core = dp // 4, lax.rem(dp // 2, 2), lax.rem(dp, 2)
    y, zh = ctx // 2, lax.rem(ctx, 2)
    me = x * 2 + core
    mine = zl * 8 + ctx

    def near(k):
        xx, cc = lax.rem(x + k // 2, 4), lax.rem(core + k % 2, 2)
        return xx, cc, {"dp": (xx * 2 + zl) * 2 + cc}

    def far(k):
        zz = lax.rem(zl + k // 8, 2)
        yy = lax.rem(y + (k // 2) % 4, 4)
        hh = lax.rem(zh + k % 2, 2)
        cc = yy * 2 + hh
        return zz * 8 + cc, {"dp": (x * 2 + zz) * 2 + core, "ctx": cc}

    rows = pl.ds(pl.multiple_of(me * ROWS, ROWS), ROWS)
    load_v = pltpu.make_async_copy(vg_ref.at[0], vgb.at[rows], lsem.at[0])
    load_h = pltpu.make_async_copy(h_ref.at[0], hid, lsem.at[1])
    load_v.start()
    load_h.start()
    barrier = pltpu.get_barrier_semaphore()
    for k in range(1, 8):
        pl.semaphore_signal(barrier, inc=1, device_id=near(k)[2], device_id_type=MESH)
    for k in range(1, 16):
        pl.semaphore_signal(barrier, inc=1, device_id=far(k)[1], device_id_type=MESH)
    load_v.wait()
    pl.semaphore_wait(barrier, 22)

    def send_v(k):
        return pltpu.make_async_remote_copy(
            src_ref=vgb.at[rows], dst_ref=vgb.at[rows], send_sem=vs.at[k], recv_sem=vr.at[k],
            device_id=near(k)[2], device_id_type=MESH,
        )

    def send_h(k, z):
        xx, cc, to = near(k)
        block = (xx * 2 + z) * 2 + cc
        return pltpu.make_async_remote_copy(
            src_ref=ht.at[pl.ds(pl.multiple_of(block * 320, 320), 320)],
            dst_ref=hg.at[z, :, rows],
            send_sem=hs.at[k, z], recv_sem=hr.at[k, z], device_id=to, device_id_type=MESH,
        )

    for k in range(1, 8):
        send_v(k).start()
    load_h.wait()
    for j in range(40):
        ht[j * 128:(j + 1) * 128, :] = hid[:, j * 128:(j + 1) * 128].T
    for k in range(1, 8):
        for z in range(2):
            send_h(k, z).start()
    for z in range(2):
        block = (x * 2 + z) * 2 + core
        hg[z, :, rows] = ht[pl.ds(pl.multiple_of(block * 320, 320), 320), :]

    def send_w(k, p):
        t, to = far(k)
        part = pl.ds(p * 80, 80)
        return pltpu.make_async_remote_copy(
            src_ref=dws.at[t, part], dst_ref=dwr.at[k, part], send_sem=ws.at[p, k], recv_sem=wr.at[p, k],
            device_id=to, device_id_type=MESH,
        )

    for k in range(1, 8):
        send_v(k).wait_recv()
        for z in range(2):
            send_h(k, z).wait_recv()
    for p in range(4):
        res = dot(hg[...].reshape(640, SEQ), vgb[:, p * 256:(p + 1) * 256], 1, 0)
        res = res.reshape(16, 40, 256)
        res = jnp.concatenate([res[:, :, :128], res[:, :, 128:]], axis=1)
        dws[:, p * 80:(p + 1) * 80, :] = res.astype(BF16)
        for k in range(1, 16):
            send_w(k, p).start()
    for p in range(4):
        part = slice(p * 80, (p + 1) * 80)
        acc = dws[mine, part, :].astype(F32)
        for k in range(1, 16):
            send_w(k, p).wait_recv()
            acc = acc + dwr[k, part, :].astype(F32)
        out_ref[:, p * 256:p * 256 + 128] = acc[:40]
        out_ref[:, p * 256 + 128:(p + 1) * 256] = acc[40:]
    for k in range(1, 8):
        send_v(k).wait_send()
        for z in range(2):
            send_h(k, z).wait_send()
    for p in range(4):
        for k in range(1, 16):
            send_w(k, p).wait_send()


def body(hidden, q, k, v, o, do, lse, docs, order):
    anyspace = pl.BlockSpec(memory_space=pl.ANY)
    vmem = pl.BlockSpec(memory_space=pltpu.VMEM)
    smem = pl.BlockSpec(memory_space=pltpu.SMEM)
    dma = pltpu.SemaphoreType.DMA
    dq, dk, dv = pl.pallas_call(
        attention_kernel,
        out_shape=(
            jax.ShapeDtypeStruct((1, ROWS, KVH * GRP * HD), BF16),
            jax.ShapeDtypeStruct((1, ROWS, KVH * HD), BF16),
            jax.ShapeDtypeStruct((1, ROWS, KVH * HD), BF16),
        ),
        in_specs=[smem, smem, anyspace, anyspace, anyspace, anyspace, anyspace, vmem],
        out_specs=(anyspace, vmem, vmem),
        scratch_shapes=[
            pltpu.VMEM((KVH, 2, SEQ, HD), BF16),
            pltpu.VMEM((KVH, GRP * ROWS, HD), BF16),
            pltpu.VMEM((KVH, GRP * ROWS, HD), BF16),
            pltpu.VMEM((KVH, GRP * ROWS, HD), BF16),
            pltpu.VMEM((SEQ, ROWS), F32),
            pltpu.VMEM((KVH, 1, GRP * ROWS), F32),
            pltpu.VMEM((KVH, 1, GRP * ROWS), F32),
            pltpu.VMEM((KVH, 2, SEQ, HD), F32),
            pltpu.VMEM((HD, GRP * ROWS), F32),
            pltpu.VMEM((KVH, ROWS, GRP * HD), BF16),
            pltpu.VMEM((KVH, 2, 2, ROWS, HD), BF16),
            pltpu.VMEM((KVH, 2, 2, ROWS, HD), BF16),
            pltpu.VMEM((KVH, 2, 2, 2 * ROWS, HD), BF16),
            pltpu.VMEM((KVH, 2, 2, 2 * ROWS, HD), BF16),
            pltpu.VMEM((KVH, 2, ROWS, HD), F32),
            pltpu.VMEM((KVH, 2, ROWS, HD), F32),
            pltpu.VMEM((KVH, 2, ROWS, HD), F32),
            dma((10, KVH)), dma((10, KVH)), dma((4,)), dma((KVH,)),
        ],
        compiler_params=pltpu.CompilerParams(
            collective_id=0, has_side_effects=True, vmem_limit_bytes=56 * 2**20
        ),
        name="attention",
    )(docs, order, q, k, v, o, do, lse)
    dw = pl.pallas_call(
        weight_kernel,
        out_shape=jax.ShapeDtypeStruct((40, KVH * HD), F32),
        in_specs=[anyspace, anyspace],
        out_specs=vmem,
        scratch_shapes=[
            pltpu.VMEM((ROWS, 5120), BF16),
            pltpu.VMEM((5120, ROWS), BF16),
            pltpu.VMEM((2, 320, SEQ), BF16),
            pltpu.VMEM((SEQ, KVH * HD), BF16),
            pltpu.VMEM((16, 320, 128), BF16),
            pltpu.VMEM((16, 320, 128), BF16),
            dma((2,)), dma((8, 2)), dma((8, 2)), dma((8,)), dma((8,)), dma((4, 16)), dma((4, 16)),
        ],
        compiler_params=pltpu.CompilerParams(
            collective_id=1, has_side_effects=True, vmem_limit_bytes=48 * 2**20
        ),
        name="weights",
    )(hidden, dv)
    return dq, dk, dv, dw


def solution(mesh):
    placed = (P("dp", "ctx", None),) * 6 + (P("dp", None, "ctx"), P("dp", None), P("dp", None))
    return jax.shard_map(
        body,
        mesh=mesh,
        in_specs=placed,
        out_specs=(P("dp", "ctx", None),) * 3 + (P(("dp", "ctx"), None),),
        check_vma=False,
    )
```

time: 1100 us -> 163 us (0.15)
  waiting for transfers between devices: 904 us -> 0 us
  Pallas kernels: 0 us -> 155 us
  local copies, waits for them, and re-layouts: 114 us -> 6.16 us
  matrix products: 50 us -> 0 us
  other arithmetic: 16.3 us -> 0 us
  between operations: 13.8 us -> 0.68 us
    unnamed x5 -> x0, waiting for transfers between devices: 688 us -> none
    pallas_call x0 -> x2, Pallas kernels: none -> 155 us  [the longest x1 93.2 us: body(): pl.pallas_call(attention_kernel, out_shape=(jax.ShapeDtypeStruct((1, ROWS...]
    reduce_scatter x1 -> x0, waiting for transfers between devices: 113 us -> none  [body(): lax.psum_scatter(partial_rows, 'ctx', scatter_dimension=0, tiled=True)]
    all_gather x2 -> x0, waiting for transfers between devices: 103 us -> none  [the longest x1 59.1 us: body(): value_piece = lax.all_gather(attn_values[0], 'ctx', axis=0, tiled=True)]
    dot_general x21 -> x0, matrix products: 50 us -> none  [the longest x4 12.6 us: one_block(): jnp.einsum('tcgd,ncd->cgtn', grad_rows, value_block, preferred_element_ty...]
    dynamic_slice x12 -> x0, local copies, waits for them, and re-layouts: 33.2 us -> none  [the longest x8 24.1 us: one_block(): current = lax.dynamic_slice_in_dim(partial_rows, offset, block_width, 0)]
    unnamed x13 -> x10, local copies, waits for them, and re-layouts: 32.3 us -> 6.16 us
    dynamic_update_slice x8 -> x0, local copies, waits for them, and re-layouts: 24.2 us -> none  [one_block(): lax.dynamic_update_slice_in_dim(partial_rows, current + new_rows, offset, 0)]
  transfers between devices with their start and end apart: 4 -> 0, of which waited for: 4 -> 0; matrix products, arithmetic and copies ran while one was open for 2% -> 0% of each run, Pallas kernels for 0% -> 0%
where the time goes in v1:
time: 163 us; the launch traced here: 162 us
  Pallas kernels  155 us (95%)
  local copies, waits for them, and re-layouts  6.16 us (4%)
    pallas_call x1, Pallas kernels, body(): pl.pallas_call(attention_kernel, out_shape=(jax.ShapeDtypeStruct((1, ROWS...  93.2 us
    pallas_call x1, Pallas kernels, body(): pl.pallas_call(weight_kernel, out_shape=jax.ShapeDtypeStruct((40, KVH * H...  61.7 us
    unnamed x10, local copies, waits for them, and re-layouts  6.16 us

profile of v1, /device:TPU:0, one launch (start us, length us, event | category | flops | bytes accessed | tf_op | source)
XLA Modules:
  0.0 161.7 jit_solution(16346672609171112242)
XLA Ops:
  0.6 0.0 copy-start
  0.6 93.2 %attention.1 = (bf16[1,128,8192]{2,1,0:T(8,128)(2,1)}, bf16[1,128,1024]{2,1,0:T(8,128)(2,1)}, bf16[1,128,1024]{2,1,0:T(8,128)(2,1)}) custom-call(s32[1,8]{1,0:T(1,128)} %doc_ref.1, s32[1,16]{1,0:T(1,128)} %ord_ref.1, bf16[1,128,8192]{2,1,0:T(8,128)(2,1)} %q_ref.1, bf16[1,128,1024]{2,1,0:T(8,128)(2,1)} %k_ref.1, bf16[1,128,1024]{2,1,0:T(8,128)(2,1)} %v_ref.1, ...), custom_call_target="tpu_custom_call" | custom-call | tf_op jit(solution)/shard_map/attention/pallas_call | solution.py:363
  93.9 0.0 copy-done
  93.9 0.0 copy-start.1
  93.9 0.9 copy-done.1
  94.8 61.7 %weights.1 = f32[40,1024]{1,0:T(8,128)S(1)} custom-call(bf16[1,128,5120]{2,1,0:T(8,128)(2,1)S(1)} %copy-done, bf16[1,128,1024]{2,1,0:T(8,128)(2,1)S(1)} %copy-done.1), custom_call_target="tpu_custom_call" | custom-call | tf_op jit(solution)/shard_map/weights/pallas_call | solution.py:397
  156.5 0.0 copy-start.2
  156.5 3.1 %copy.17 = bf16[1,128,8192]{2,1,0:T(8,128)(2,1)} copy(bf16[1,128,8192]{2,1,0:T(8,128)(2,1)} %get-tuple-element.14) | data formatting | bytes 4194304
  159.6 0.0 copy-done.2
  159.6 0.7 copy.18
  160.3 0.7 copy.19
  161.1 0.7 copy.20
Async XLA Ops:
  0.6 93.2 %copy-start = (bf16[1,128,5120]{2,1,0:T(8,128)(2,1)S(1)}, bf16[1,128,5120]{2,1,0:T(8,128)(2,1)}, u32[]{:S(2)}) copy-start(bf16[1,128,5120]{2,1,0:T(8,128)(2,1)} %h_ref.1) | copy-start | bytes 3932164
  93.9 1.0 copy-start.1
  156.5 3.1 %copy-start.2 = (bf16[1,128,1024]{2,1,0:T(8,128)(2,1)S(1)}, bf16[1,128,1024]{2,1,0:T(8,128)(2,1)}, u32[]{:S(2)}) copy-start(bf16[1,128,1024]{2,1,0:T(8,128)(2,1)} %get-tuple-element.15) | copy-start | bytes 786436

commit v2 on v1

v2 whole, which is shorter than its diff:
```python
import math

import jax
import jax.numpy as jnp
from jax import lax
from jax.experimental import pallas as pl
from jax.experimental.pallas import tpu as pltpu
from jax.sharding import PartitionSpec as P

MESH = pl.DeviceIdType.MESH
F32 = jnp.float32
BF16 = jnp.bfloat16
KVH = 8
GRP = 8
HD = 128
ROWS = 128
SEQ = 1024
SCALE = HD ** (-0.5)
LOG2E = math.log2(math.e)
BIG = 3.0e38
NB = 256

A0, A1P, A1M, A3P, A3M = range(5)
V1P, V1M, V2P, V2M, Z0, ZP, ZM, ZO = range(5, 13)
B1P, B1M, B2P, B2M, B3 = range(13, 18)
W0, W1P, W1M, W2P, W2M = range(18, 23)
KINDS = 23


def dot(a, b, ca, cb):
    return lax.dot_general(a, b, (((ca,), (cb,)), ((), ())), preferred_element_type=F32)


def rng(start, size):
    return pl.ds(pl.multiple_of(start, size), size)


def kernel(
    doc_ref, ord_ref, q_ref, k_ref, v_ref, o_ref, do_ref, lse_ref, h_ref,
    dq_ref, dk_ref, dv_ref, dw_ref,
    kvb, qb, dob, ob, cap, lser, deltar, pf, dqt, dqs,
    s1, r1, s2, r2, s3, r3, fin, w0s, w0r, w1s, w1r, w2s, w2r,
    hid, ht, hg, vgb, dws, dwr,
    send, recv, lsem, dqsem, hs, hr, vs, vr, ws, wr,
):
    dp, ctx = lax.axis_index("dp"), lax.axis_index("ctx")
    x, zl, core = dp // 4, lax.rem(dp // 2, 2), lax.rem(dp, 2)
    y, zh = ctx // 2, lax.rem(ctx, 2)
    partner = y * 2 + 1 - zh
    yp, ym, yo = lax.rem(y + 1, 4), lax.rem(y + 3, 4), lax.rem(y + 2, 4)
    up, down = yp * 2 + zh, ym * 2 + zh
    me = x * 2 + core
    mine = zl * 8 + ctx

    def load_kv(g, c):
        cols, rows = rng(g * HD, HD), rng(ctx * ROWS, ROWS)
        pltpu.make_async_copy(k_ref.at[0, :, cols], kvb.at[g, 0, rows], lsem.at[0]).start()
        pltpu.make_async_copy(v_ref.at[0, :, cols], kvb.at[g, 1, rows], lsem.at[0]).start()
        return c

    lax.fori_loop(0, KVH, load_kv, 0)

    def load_heads(h, c):
        cols = rng(h * HD, HD)
        g = h // GRP
        rows = rng(lax.rem(h, GRP) * ROWS, ROWS)
        pltpu.make_async_copy(do_ref.at[0, :, cols], dob.at[g, rows], lsem.at[1]).start()
        pltpu.make_async_copy(o_ref.at[0, :, cols], ob.at[g, rows], lsem.at[2]).start()
        pltpu.make_async_copy(q_ref.at[0, :, cols], qb.at[g, rows], lsem.at[3]).start()
        return c

    lax.fori_loop(0, KVH * GRP, load_heads, 0)
    load_hidden = pltpu.make_async_copy(h_ref.at[0], hid, lsem.at[4])
    load_hidden.start()

    def near(k):
        xx, cc = lax.rem(x + k // 2, 4), lax.rem(core + lax.rem(k, 2), 2)
        return xx, cc, {"dp": (xx * 2 + zl) * 2 + cc}

    def far(k):
        zz = lax.rem(zl + k // 8, 2)
        yy = lax.rem(y + lax.rem(k // 2, 4), 4)
        cc = yy * 2 + lax.rem(zh + lax.rem(k, 2), 2)
        return zz * 8 + cc, {"dp": (x * 2 + zz) * 2 + core, "ctx": cc}

    barrier = pltpu.get_barrier_semaphore()
    for k in range(1, 8):
        pl.semaphore_signal(barrier, inc=1, device_id=near(k)[2], device_id_type=MESH)
    for k in range(1, 16):
        pl.semaphore_signal(barrier, inc=1, device_id=far(k)[1], device_id_type=MESH)
    own = rng(ctx * ROWS, ROWS)
    pltpu.make_async_copy(kvb.at[:, :, own], kvb.at[:, :, own], lsem.at[0]).wait()
    pl.semaphore_wait(barrier, 22)

    def slot(s):
        return rng(s * 2 * ROWS, 2 * ROWS)

    def half(s, z):
        return rng((s * 2 + z) * ROWS, ROWS)

    def quarter(s, z, n):
        return rng((s * 4 + z * 2 + n) * 64, 64)

    def msg(kind, g):
        same = {
            A0: (0, own, partner),
            A1P: (0, slot(y), up),
            A1M: (0, slot(y), down),
            A3P: (0, half(ym, 0), up),
            A3M: (0, half(yp, 1), down),
            V1P: (1, own, up),
            V1M: (1, own, down),
            V2P: (1, quarter(ym, zh, 0), up),
            V2M: (1, quarter(yp, zh, 1), down),
            Z0: (1, own, partner),
            ZP: (1, half(yp, zh), partner),
            ZM: (1, half(ym, zh), partner),
            ZO: (1, half(yo, zh), partner),
        }
        other = {
            B1P: (s1.at[g, 0], r1.at[g, 0], up),
            B1M: (s1.at[g, 1], r1.at[g, 1], down),
            B2P: (s2.at[g, 0], r2.at[g, 0], up),
            B2M: (s2.at[g, 1], r2.at[g, 1], down),
            B3: (s3.at[g], r3.at[g], partner),
            W0: (w0s.at[g], w0r.at[g], partner),
            W1P: (w1s.at[g, 0], w1r.at[g, 0], up),
            W1M: (w1s.at[g, 1], w1r.at[g, 1], down),
            W2P: (w2s.at[g, 0], w2r.at[g, 0], up),
            W2M: (w2s.at[g, 1], w2r.at[g, 1], down),
        }
        if kind in same:
            which, rows, to = same[kind]
            src = dst = kvb.at[g, which, rows]
        else:
            src, dst, to = other[kind]
        return pltpu.make_async_remote_copy(
            src_ref=src, dst_ref=dst, send_sem=send.at[kind, g], recv_sem=recv.at[kind, g],
            device_id={"ctx": to}, device_id_type=MESH,
        )

    def go(g, *kinds):
        for kind in kinds:
            msg(kind, g).start()

    def take(g, *kinds):
        for kind in kinds:
            msg(kind, g).wait_recv()

    def gather0(g):
        go(g, A0, V1P, V1M, Z0)

    def gather1(g):
        take(g, A0)
        go(g, A1P, A1M)
        take(g, V1P)
        go(g, V2P, ZM)
        take(g, V1M)
        go(g, V2M, ZP)

    def gather2(g):
        take(g, A1P)
        go(g, A3P)
        take(g, A1M)
        go(g, A3M)
        take(g, V2P, V2M)
        go(g, ZO)

    for g in range(3):
        gather0(g)

    lane = lax.broadcasted_iota(jnp.int32, (1, ROWS), 1)
    pos_q = jnp.where(
        lane < 64, ord_ref[0, 2 * ctx] * 64 + lane, ord_ref[0, 2 * ctx + 1] * 64 + lane - 64
    )
    start_q = jnp.zeros((1, ROWS), jnp.int32)
    end = jnp.int32(0)
    for j in range(8):
        end = end + doc_ref[0, j]
        start_q = jnp.where(pos_q >= end, end, start_q)
    for j in range(16):
        pos_n = ord_ref[0, j] * 64 + lax.broadcasted_iota(jnp.int32, (64, ROWS), 0)
        seen = (pos_n <= pos_q) & (pos_n >= start_q)
        cap[j * 64:(j + 1) * 64, :] = jnp.where(seen, BIG, -BIG)

    gather1(0)
    gather1(1)
    for n in (1, 2, 3):
        ref = (dob, ob, qb)[n - 1]
        pltpu.make_async_copy(ref, ref, lsem.at[n]).wait()
    load_hidden.wait()
    gather2(0)

    def rows_of(g):
        heads = lse_ref[0, rng(g * GRP, GRP), :] * LOG2E
        for h in range(GRP):
            cols = slice(h * ROWS, (h + 1) * ROWS)
            prod = dob[g, cols, :].astype(F32) * ob[g, cols, :].astype(F32)
            deltar[g, :, cols] = jnp.sum(prod.T, axis=0, keepdims=True)
            lser[g, :, cols] = heads[h:h + 1, :]

    def compute(g):
        dqt[...] = jnp.zeros_like(dqt)

        def keys(nb, c):
            r = rng(nb * NB, NB)
            kk, vv = kvb[g, 0, r, :], kvb[g, 1, r, :]
            top = cap[r, :]
            top = jnp.concatenate([top, top], axis=1)
            dk = dv = None
            for hp in range(4):
                cols = slice(hp * 256, (hp + 1) * 256)
                qq, dd = qb[g, cols, :], dob[g, cols, :]
                st = dot(kk, qq, 1, 1)
                p = jnp.exp2(jnp.minimum(st * (SCALE * LOG2E) - lser[g, :, cols], top))
                dp_ = dot(vv, dd, 1, 1)
                ds = (p * (dp_ - deltar[g, :, cols]) * SCALE).astype(BF16)
                pv, pk = dot(p.astype(BF16), dd, 1, 0), dot(ds, qq, 1, 0)
                dv, dk = (pv, pk) if dv is None else (dv + pv, dk + pk)
                dqt[:, cols] += dot(kk, ds, 0, 0)
            pf[g, 0, r, :] = dk
            pf[g, 1, r, :] = dv
            return c

        lax.fori_loop(0, SEQ // NB, keys, 0)
        for h in range(GRP):
            cols = slice(h * ROWS, (h + 1) * ROWS)
            dqs[g, :, cols] = dqt[:, cols].T.astype(BF16)
        dq_copy(g).start()

    def dq_copy(g):
        return pltpu.make_async_copy(dqs.at[g], dq_ref.at[0, :, rng(g * GRP * HD, GRP * HD)], dqsem.at[g])

    def sum1(g):
        s1[g, 0] = pf[g, 0, half(yo, 0), :].astype(BF16)
        s1[g, 1] = pf[g, 0, half(yo, 1), :].astype(BF16)
        go(g, B1P, B1M)
        for s in range(4):
            w0s[g, s] = pf[g, 1, half(s, 1 - zh), :].astype(BF16)
        go(g, W0)

    def sum2(g):
        s2[g, 0, ROWS:, :] = pf[g, 0, half(yp, 1), :].astype(BF16)
        s2[g, 1, :ROWS, :] = pf[g, 0, half(ym, 0), :].astype(BF16)
        take(g, B1P)
        s2[g, 0, :ROWS, :] = (pf[g, 0, half(yp, 0), :] + r1[g, 0].astype(F32)).astype(BF16)
        go(g, B2P)
        take(g, B1M)
        s2[g, 1, ROWS:, :] = (pf[g, 0, half(ym, 1), :] + r1[g, 1].astype(F32)).astype(BF16)
        go(g, B2M)
        take(g, W0)
        for s in range(4):
            pf[g, 1, half(s, zh), :] += w0r[g, s].astype(F32)
        w1s[g, 0] = pf[g, 1, quarter(yo, zh, 0), :].astype(BF16)
        w1s[g, 1] = pf[g, 1, quarter(yo, zh, 1), :].astype(BF16)
        go(g, W1P, W1M)

    def sum3(g):
        w2s[g, 0, 64:, :] = pf[g, 1, quarter(yp, zh, 1), :].astype(BF16)
        w2s[g, 1, :64, :] = pf[g, 1, quarter(ym, zh, 0), :].astype(BF16)
        take(g, W1P)
        w2s[g, 0, :64, :] = (pf[g, 1, quarter(yp, zh, 0), :] + w1r[g, 0].astype(F32)).astype(BF16)
        go(g, W2P)
        take(g, W1M)
        w2s[g, 1, 64:, :] = (pf[g, 1, quarter(ym, zh, 1), :] + w1r[g, 1].astype(F32)).astype(BF16)
        go(g, W2M)
        take(g, B2P, B2M)

        def total(z):
            rows = rng(z * ROWS, ROWS)
            return pf[g, 0, half(y, z), :] + r2[g, 0, rows, :].astype(F32) + r2[g, 1, rows, :].astype(F32)

        s3[g] = total(1 - zh).astype(BF16)
        go(g, B3)
        fin[g] = total(zh)

    def sum4(g):
        cols = rng(g * HD, HD)
        take(g, W2P, W2M)
        dv = (pf[g, 1, own, :] + w2r[g, 0].astype(F32) + w2r[g, 1].astype(F32)).astype(BF16)
        dv_ref[0, :, cols] = dv
        vgb[g // 2, rng(me * ROWS, ROWS), rng(lax.rem(g, 2) * HD, HD)] = dv
        take(g, B3)
        dk_ref[0, :, cols] = (fin[g] + r3[g].astype(F32)).astype(BF16)

    def send_h(k, z):
        xx, cc, to = near(k)
        return pltpu.make_async_remote_copy(
            src_ref=ht.at[rng(((xx * 2 + z) * 2 + cc) * 320, 320)],
            dst_ref=hg.at[z, :, rng(me * ROWS, ROWS)],
            send_sem=hs.at[k, z], recv_sem=hr.at[k, z], device_id=to, device_id_type=MESH,
        )

    def turn(i):
        dx, z = i // 2, lax.rem(i, 2)
        j = lax.rem(x + dx, 4) * 2 + z
        for n in range(5):
            at = j * 640 + n * 128
            ht[rng(at, 128), :] = hid[:, rng(at, 128)].T
        send_h(dx * 2 + 1, z).start()

        @pl.when(dx > 0)
        def _():
            send_h(dx * 2, z).start()

        @pl.when(dx == 0)
        def _():
            hg[z, :, rng(me * ROWS, ROWS)] = ht[rng((j * 2 + core) * 320, 320), :]

    def send_v(k, p):
        rows = rng(me * ROWS, ROWS)
        return pltpu.make_async_remote_copy(
            src_ref=vgb.at[p, rows], dst_ref=vgb.at[p, rows], send_sem=vs.at[p, k], recv_sem=vr.at[p, k],
            device_id=near(k)[2], device_id_type=MESH,
        )

    def send_w(k, p):
        t, to = far(k)
        return pltpu.make_async_remote_copy(
            src_ref=dws.at[p, t], dst_ref=dwr.at[p, k], send_sem=ws.at[p, k], recv_sem=wr.at[p, k],
            device_id=to, device_id_type=MESH,
        )

    def each(lo, hi, f):
        def one(k, c):
            f(k)
            return c

        lax.fori_loop(lo, hi, one, 0)

    def weights1(p):
        each(1, 8, lambda k: send_v(k, p).start())

    def weights2(p):
        @pl.when(p == 0)
        def _():
            def arrived(k):
                send_h(k, 0).wait_recv()
                send_h(k, 1).wait_recv()

            each(1, 8, arrived)

        each(1, 8, lambda k: send_v(k, p).wait_recv())
        res = dot(hg[...].reshape(640, SEQ), vgb[p], 1, 0).reshape(16, 40, 256)
        dws[p] = jnp.concatenate([res[:, :, :128], res[:, :, 128:]], axis=1).astype(BF16)
        each(1, 16, lambda k: send_w(k, p).start())

    def weights3(p):
        each(1, 16, lambda k: send_w(k, p).wait_recv())
        acc = dws[p, mine].astype(F32)
        for k in range(1, 16):
            acc = acc + dwr[p, k].astype(F32)
        dw_ref[:, rng(p * 256, 128)] = acc[:40]
        dw_ref[:, rng(p * 256 + 128, 128)] = acc[40:]

    def at(i, lo, count, f):
        @pl.when((i >= lo) & (i < lo + count))
        def _():
            f(i - lo)

    def at_pair(i, lo, f):
        @pl.when((i >= lo) & (i < lo + 8) & (lax.rem(i - lo, 2) == 0))
        def _():
            f((i - lo) // 2)

    def step(i, c):
        at(i, -3, KVH, gather0)
        at(i, -2, KVH, gather1)
        at(i, -1, KVH, gather2)

        @pl.when(i < KVH)
        def _():
            @pl.when(i < 4)
            def _():
                turn(2 * i)
                turn(2 * i + 1)

            rows_of(i)
            take(i, A3P, A3M, Z0, ZP, ZM, ZO)
            compute(i)
            sum1(i)

        at(i, 1, KVH, sum2)
        at(i, 2, KVH, sum3)
        at(i, 3, KVH, sum4)
        at_pair(i, 4, weights1)
        at_pair(i, 5, weights2)
        at_pair(i, 7, weights3)
        return c

    lax.fori_loop(0, 14, step, 0)

    def finish(g, c):
        for kind in range(KINDS):
            msg(kind, g).wait_send()
        dq_copy(g).wait()
        return c

    lax.fori_loop(0, KVH, finish, 0)

    def sent_near(k):
        for z in range(2):
            send_h(k, z).wait_send()
        for p in range(4):
            send_v(k, p).wait_send()

    def sent_far(k):
        for p in range(4):
            send_w(k, p).wait_send()

    each(1, 8, sent_near)
    each(1, 16, sent_far)


def body(hidden, q, k, v, o, do, lse, docs, order):
    anyspace = pl.BlockSpec(memory_space=pl.ANY)
    vmem = pl.BlockSpec(memory_space=pltpu.VMEM)
    smem = pl.BlockSpec(memory_space=pltpu.SMEM)
    dma = pltpu.SemaphoreType.DMA
    return pl.pallas_call(
        kernel,
        out_shape=(
            jax.ShapeDtypeStruct((1, ROWS, KVH * GRP * HD), BF16),
            jax.ShapeDtypeStruct((1, ROWS, KVH * HD), BF16),
            jax.ShapeDtypeStruct((1, ROWS, KVH * HD), BF16),
            jax.ShapeDtypeStruct((40, KVH * HD), F32),
        ),
        in_specs=[smem, smem] + [anyspace] * 5 + [vmem, anyspace],
        out_specs=(anyspace, vmem, vmem, vmem),
        scratch_shapes=[
            pltpu.VMEM((KVH, 2, SEQ, HD), BF16),
            pltpu.VMEM((KVH, GRP * ROWS, HD), BF16),
            pltpu.VMEM((KVH, GRP * ROWS, HD), BF16),
            pltpu.VMEM((KVH, GRP * ROWS, HD), BF16),
            pltpu.VMEM((SEQ, ROWS), F32),
            pltpu.VMEM((KVH, 1, GRP * ROWS), F32),
            pltpu.VMEM((KVH, 1, GRP * ROWS), F32),
            pltpu.VMEM((KVH, 2, SEQ, HD), F32),
            pltpu.VMEM((HD, GRP * ROWS), F32),
            pltpu.VMEM((KVH, ROWS, GRP * HD), BF16),
            pltpu.VMEM((KVH, 2, ROWS, HD), BF16),
            pltpu.VMEM((KVH, 2, ROWS, HD), BF16),
            pltpu.VMEM((KVH, 2, 2 * ROWS, HD), BF16),
            pltpu.VMEM((KVH, 2, 2 * ROWS, HD), BF16),
            pltpu.VMEM((KVH, ROWS, HD), BF16),
            pltpu.VMEM((KVH, ROWS, HD), BF16),
            pltpu.VMEM((KVH, ROWS, HD), F32),
            pltpu.VMEM((KVH, 4, ROWS, HD), BF16),
            pltpu.VMEM((KVH, 4, ROWS, HD), BF16),
            pltpu.VMEM((KVH, 2, 64, HD), BF16),
            pltpu.VMEM((KVH, 2, 64, HD), BF16),
            pltpu.VMEM((KVH, 2, ROWS, HD), BF16),
            pltpu.VMEM((KVH, 2, ROWS, HD), BF16),
            pltpu.VMEM((ROWS, 5120), BF16),
            pltpu.VMEM((5120, ROWS), BF16),
            pltpu.VMEM((2, 320, SEQ), BF16),
            pltpu.VMEM((4, SEQ, 256), BF16),
            pltpu.VMEM((4, 16, 80, 128), BF16),
            pltpu.VMEM((4, 16, 80, 128), BF16),
            dma((KINDS, KVH)), dma((KINDS, KVH)), dma((5,)), dma((KVH,)),
            dma((8, 2)), dma((8, 2)), dma((4, 8)), dma((4, 8)), dma((4, 16)), dma((4, 16)),
        ],
        compiler_params=pltpu.CompilerParams(
            collective_id=0, has_side_effects=True, vmem_limit_bytes=56 * 2**20
        ),
        name="attention_and_weights",
    )(docs, order, q, k, v, o, do, lse, hidden)


def solution(mesh):
    placed = (P("dp", "ctx", None),) * 6 + (P("dp", None, "ctx"), P("dp", None), P("dp", None))
    return jax.shard_map(
        body,
        mesh=mesh,
        in_specs=placed,
        out_specs=(P("dp", "ctx", None),) * 3 + (P(("dp", "ctx"), None),),
        check_vma=False,
    )
```

time: 163 us -> 118 us (0.72)
  Pallas kernels: 155 us -> 112 us
    pallas_call x2 -> x1, Pallas kernels: 155 us -> 112 us  [body(): pl.pallas_call(kernel, out_shape=(jax.ShapeDtypeStruct((1, ROWS, KVH * GR...]
where the time goes in v2:
time: 118 us
  Pallas kernels  112 us (95%)
  local copies, waits for them, and re-layouts  5.24 us (4%)
    pallas_call x1, Pallas kernels, body(): pl.pallas_call(kernel, out_shape=(jax.ShapeDtypeStruct((1, ROWS, KVH * GR...  112 us
    unnamed x10, local copies, waits for them, and re-layouts  5.24 us

profile of v2, /device:TPU:0, one launch (start us, length us, event | category | flops | bytes accessed | tf_op | source)
XLA Modules:
  0.0 117.7 jit_solution(4000241471938865467)
XLA Ops:
  0.6 111.8 %attention_and_weights.1 = (bf16[1,128,8192]{2,1,0:T(8,128)(2,1)}, bf16[1,128,1024]{2,1,0:T(8,128)(2,1)}, bf16[1,128,1024]{2,1,0:T(8,128)(2,1)}, f32[40,1024]{1,0:T(8,128)}) custom-call(s32[1,8]{1,0:T(1,128)} %doc_ref.1, s32[1,16]{1,0:T(1,128)} %ord_ref.1, bf16[1,128,8192]{2,1,0:T(8,128)(2,1)} %q_ref.1, bf16[1,128,1024]{2,1,0:T(8,128)(2,1)} %k_ref.1, ...), custom_call_target="tpu_custom_call" | custom-call | tf_op jit(solution)/shard_map/attention_and_weights/pallas_call | solution.py:420
  112.5 0.0 copy-start.1
  112.5 0.0 copy-start
  112.5 0.0 copy-start.2
  112.5 3.2 %copy.17 = bf16[1,128,8192]{2,1,0:T(8,128)(2,1)} copy(bf16[1,128,8192]{2,1,0:T(8,128)(2,1)} %get-tuple-element.8) | data formatting | bytes 4194304
  115.7 0.0 copy-done.1
  115.7 0.7 copy.18
  116.4 0.0 copy-done
  116.4 0.7 copy.19
  117.1 0.0 copy-done.2
  117.1 0.7 copy.20
Async XLA Ops:
  112.5 3.2 %copy-start.1 = (bf16[1,128,1024]{2,1,0:T(8,128)(2,1)S(1)}, bf16[1,128,1024]{2,1,0:T(8,128)(2,1)}, u32[]{:S(2)}) copy-start(bf16[1,128,1024]{2,1,0:T(8,128)(2,1)} %get-tuple-element.9) | copy-start | bytes 786436
  112.5 3.9 %copy-start = (bf16[1,128,1024]{2,1,0:T(8,128)(2,1)S(1)}, bf16[1,128,1024]{2,1,0:T(8,128)(2,1)}, u32[]{:S(2)}) copy-start(bf16[1,128,1024]{2,1,0:T(8,128)(2,1)} %get-tuple-element.10) | copy-start | bytes 786436
  112.5 4.6 %copy-start.2 = (f32[40,1024]{1,0:T(8,128)S(1)}, f32[40,1024]{1,0:T(8,128)}, u32[]{:S(2)}) copy-start(f32[40,1024]{1,0:T(8,128)} %get-tuple-element.11) | copy-start | bytes 491524

commit v3 on v2

v3 whole, which is shorter than its diff:
```python
import math

import jax
import jax.numpy as jnp
from jax import lax
from jax.experimental import pallas as pl
from jax.experimental.pallas import tpu as pltpu
from jax.sharding import PartitionSpec as P

MESH = pl.DeviceIdType.MESH
F32 = jnp.float32
BF16 = jnp.bfloat16
KVH = 8
GRP = 8
HD = 128
ROWS = 128
SEQ = 1024
SCALE = HD ** (-0.5)
LOG2E = math.log2(math.e)
BIG = 3.0e38
NB = 1024
K1, K2, V0, V1, V2 = -6, -3, 0, 3, 6
D2, D3, D4 = 3, 6, 8
E2, E3, E4 = 11, 14, 17
G1, G2, G3, G4 = 9, 12, 14, 16

A0, A1P, A1M, A3P, A3M = range(5)
V1P, V1M, V2P, V2M, Z0, ZP, ZM, ZO = range(5, 13)
B1P, B1M, B2P, B2M, B3 = range(13, 18)
W0, W1P, W1M, W2P, W2M = range(18, 23)
SEM = (0, 1, 1, 2, 2) + (0, 0, 1, 1, 2, 2, 2, 2) + (3, 3, 4, 4, 5) + (3, 4, 4, 5, 5)
SENT = 896


def dot(a, b, ca, cb):
    return lax.dot_general(a, b, (((ca,), (cb,)), ((), ())), preferred_element_type=F32)


def rng(start, size):
    return pl.ds(pl.multiple_of(start, size), size)


def kernel(
    doc_ref, ord_ref, q_ref, k_ref, v_ref, o_ref, do_ref, lse_ref, h_ref,
    dq_ref, dk_ref, dv_ref, dw_ref,
    kvb, qb, dob, ob, cap, lser, deltar, pf, dqt, probs, lse,
    s1, r1, s2, r2, s3, r3, fin, w0s, w0r, w1s, w1r, w2s, w2r,
    hid, ht, hg, vgb, dws, dwr, dus, dur,
    send, recv, lsem, hsem, dqsem, hs, hr, vs, vr, ws, wr, us, ur,
):
    dp, ctx = lax.axis_index("dp"), lax.axis_index("ctx")
    x, zl, core = dp // 4, lax.rem(dp // 2, 2), lax.rem(dp, 2)
    y, zh = ctx // 2, lax.rem(ctx, 2)
    partner = y * 2 + 1 - zh
    yp, ym, yo = lax.rem(y + 1, 4), lax.rem(y + 3, 4), lax.rem(y + 2, 4)
    up, down = yp * 2 + zh, ym * 2 + zh
    me = x * 2 + core
    mine = zl * 2 + zh

    def near(k):
        xx, cc = lax.rem(x + k // 2, 4), lax.rem(core + lax.rem(k, 2), 2)
        return xx, cc, {"dp": (xx * 2 + zl) * 2 + cc}

    def along_y(k):
        yy = lax.rem(y + k, 4)
        return yy, {"ctx": yy * 2 + zh}

    def along_z(k):
        zz, hh = lax.rem(zl + k // 2, 2), lax.rem(zh + lax.rem(k, 2), 2)
        return zz * 2 + hh, {"dp": (x * 2 + zz) * 2 + core, "ctx": y * 2 + hh}

    barrier = pltpu.get_barrier_semaphore()
    for k in range(1, 8):
        pl.semaphore_signal(barrier, inc=1, device_id=near(k)[2], device_id_type=MESH)
    for k in range(1, 4):
        pl.semaphore_signal(barrier, inc=1, device_id=along_y(k)[1], device_id_type=MESH)
        pl.semaphore_signal(barrier, inc=1, device_id=along_z(k)[1], device_id_type=MESH)
    def load_kv(g, c):
        cols, rows = rng(g * HD, HD), rng(ctx * ROWS, ROWS)
        pltpu.make_async_copy(k_ref.at[0, :, cols], kvb.at[g, 0, rows], lsem.at[0]).start()
        pltpu.make_async_copy(v_ref.at[0, :, cols], kvb.at[g, 1, rows], lsem.at[0]).start()
        return c

    lax.fori_loop(0, KVH, load_kv, 0)

    own = rng(ctx * ROWS, ROWS)
    pltpu.make_async_copy(kvb.at[:, :, own], kvb.at[:, :, own], lsem.at[0]).wait()
    pl.semaphore_wait(barrier, 13)

    def slot(s):
        return rng(s * 2 * ROWS, 2 * ROWS)

    def half(s, z):
        return rng((s * 2 + z) * ROWS, ROWS)

    def quarter(s, z, n):
        return rng((s * 4 + z * 2 + n) * 64, 64)

    def msg(kind, w, g):
        same = {
            A0: (own, partner),
            A1P: (slot(y), up),
            A1M: (slot(y), down),
            A3P: (half(ym, 0), up),
            A3M: (half(yp, 1), down),
            V1P: (own, up),
            V1M: (own, down),
            V2P: (quarter(ym, zh, 0), up),
            V2M: (quarter(yp, zh, 1), down),
            Z0: (own, partner),
            ZP: (half(yp, zh), partner),
            ZM: (half(ym, zh), partner),
            ZO: (half(yo, zh), partner),
        }
        j = w * 4 + g // 2
        other = {
            B1P: (s1.at[j, 0], r1.at[j, 0], up),
            B1M: (s1.at[j, 1], r1.at[j, 1], down),
            B2P: (s2.at[j, 0], r2.at[j, 0], up),
            B2M: (s2.at[j, 1], r2.at[j, 1], down),
            B3: (s3.at[j], r3.at[j], partner),
            W0: (w0s.at[j], w0r.at[j], partner),
            W1P: (w1s.at[j, 0], w1r.at[j, 0], up),
            W1M: (w1s.at[j, 1], w1r.at[j, 1], down),
            W2P: (w2s.at[j, 0], w2r.at[j, 0], up),
            W2M: (w2s.at[j, 1], w2r.at[j, 1], down),
        }
        if kind in same:
            rows, to = same[kind]
            src = dst = kvb.at[g, w, rows]
        else:
            src, dst, to = other[kind]
        return pltpu.make_async_remote_copy(
            src_ref=src, dst_ref=dst, send_sem=send.at[w, kind // 13], recv_sem=recv.at[SEM[kind], w * KVH + g],
            device_id={"ctx": to}, device_id_type=MESH,
        )

    def go(w, g, *kinds):
        for kind in kinds:
            msg(kind, w, g).start()

    def take(w, g, kind, rows):
        whole = kvb.at[g, w, pl.ds(0, rows)]
        pltpu.make_async_copy(whole, whole, recv.at[SEM[kind], w * KVH + g]).wait()

    def wait(ref, sem):
        pltpu.make_async_copy(ref, ref, sem).wait()

    def each(lo, hi, f):
        def one(k, c):
            f(k)
            return c

        lax.fori_loop(lo, hi, one, 0)

    def either(w, first, second):
        def run(g):
            even = lax.rem(g + w, 2) == 0

            @pl.when(even)
            def _():
                first(w, g)

            @pl.when(jnp.logical_not(even))
            def _():
                second(w, g)

        return run

    def zy0(w, g):
        go(w, g, A0)

    def zy1(w, g):
        take(w, g, A0, ROWS)
        go(w, g, A1P, A1M)

    def zy2(w, g):
        take(w, g, A1P, 4 * ROWS)
        go(w, g, A3P, A3M)

    def zy3(w, g):
        take(w, g, A3P, 2 * ROWS)

    def yz0(w, g):
        go(w, g, V1P, V1M, Z0)

    def yz1(w, g):
        take(w, g, V1P, 2 * ROWS)
        go(w, g, V2P, V2M, ZM, ZP)

    def yz2(w, g):
        take(w, g, V2P, ROWS)
        go(w, g, ZO)

    def yz3(w, g):
        take(w, g, Z0, 4 * ROWS)

    keys = [either(0, *two) for two in ((zy0, yz0), (zy1, yz1), (zy2, yz2), (zy3, yz3))]
    values = [either(1, *two) for two in ((zy0, yz0), (zy1, yz1), (zy2, yz2), (zy3, yz3))]

    each(0, KVH, keys[0])

    load_lse = pltpu.make_async_copy(lse_ref.at[0], lse, lsem.at[2])
    load_lse.start()
    load_hidden = pltpu.make_async_copy(h_ref.at[0], hid, lsem.at[1])
    load_hidden.start()

    def load_heads(g):
        cols = rng(g * GRP * HD, GRP * HD)
        return [
            pltpu.make_async_copy(ref.at[0, :, cols], buf.at[g], hsem.at[g])
            for ref, buf in ((do_ref, dob), (o_ref, ob), (q_ref, qb))
        ]

    def start_heads(g, c):
        for copy in load_heads(g):
            copy.start()
        return c

    lax.fori_loop(0, KVH, start_heads, 0)

    lane = lax.broadcasted_iota(jnp.int32, (1, ROWS), 1)
    pos_q = jnp.where(
        lane < 64, ord_ref[0, 2 * ctx] * 64 + lane, ord_ref[0, 2 * ctx + 1] * 64 + lane - 64
    )
    start_q = jnp.zeros((1, ROWS), jnp.int32)
    end = jnp.int32(0)
    for j in range(8):
        end = end + doc_ref[0, j]
        start_q = jnp.where(pos_q >= end, end, start_q)
    for j in range(16):
        pos_n = ord_ref[0, j] * 64 + lax.broadcasted_iota(jnp.int32, (64, ROWS), 0)
        seen = (pos_n <= pos_q) & (pos_n >= start_q)
        cap[j * 64:(j + 1) * 64, :] = jnp.where(seen, BIG, -BIG)

    each(0, -K1, keys[1])
    each(0, -V0, values[0])
    load_hidden.wait()
    load_lse.wait()
    each(0, -K2, keys[2])
    each(0, -V1, values[1])
    each(0, -V2, values[2])

    def rows_of(g):
        wait(kvb.at[pl.ds(0, 3), 0], hsem.at[g])
        heads = lse[rng(g * GRP, GRP), :] * LOG2E
        for h in range(GRP):
            cols = slice(h * ROWS, (h + 1) * ROWS)
            prod = dob[g, :, cols].astype(F32) * ob[g, :, cols].astype(F32)
            deltar[g, :, cols] = jnp.sum(prod.T, axis=0, keepdims=True) * SCALE
            lser[g, :, cols] = heads[h:h + 1, :]

    def stack(ref, g):
        return jnp.concatenate([ref[g, :, h * HD:(h + 1) * HD] for h in range(GRP)], axis=0)

    def pass1(g):
        qq, dd = stack(qb, g), stack(dob, g)

        def block(nb, c):
            r = rng(nb * NB, NB)
            top = jnp.concatenate([cap[r, :]] * GRP, axis=1)
            st = dot(kvb[g, 0, r, :], qq, 1, 1)
            p = jnp.exp2(jnp.minimum(st * (SCALE * LOG2E) - lser[g], top)).astype(BF16)
            probs[g, r, :] = p
            pf[g, r, :] = dot(p, dd, 1, 0)
            return c

        lax.fori_loop(0, SEQ // NB, block, 0)

    def pass2(g):
        qq, dd = stack(qb, g), stack(dob, g)

        def block(nb):
            r = rng(nb * NB, NB)
            dp_ = dot(kvb[g, 1, r, :], dd, 1, 1)
            ds = (probs[g, r, :].astype(F32) * (dp_ * SCALE - deltar[g])).astype(BF16)
            pf[g, r, :] = dot(ds, qq, 1, 0)
            dqt[...] = (dqt[...] if nb else 0.0) + dot(kvb[g, 0, r, :].T, ds, 1, 0)

        for nb in range(SEQ // NB):
            block(nb)
        for h in range(GRP):
            cols = slice(h * ROWS, (h + 1) * ROWS)
            ob[g, :, cols] = dqt[:, cols].T.astype(BF16)
        dq_copy(g).start()

    def dq_copy(g):
        return pltpu.make_async_copy(ob.at[g], dq_ref.at[0, :, rng(g * GRP * HD, GRP * HD)], dqsem.at[0])

    def b1(w, g):
        j = w * 4 + g // 2
        s1[j, 0] = pf[g, half(yo, 0), :].astype(BF16)
        s1[j, 1] = pf[g, half(yo, 1), :].astype(BF16)
        go(w, g, B1P, B1M)

    def b2(w, g):
        j = w * 4 + g // 2
        s2[j, 0, ROWS:, :] = pf[g, half(yp, 1), :].astype(BF16)
        s2[j, 1, :ROWS, :] = pf[g, half(ym, 0), :].astype(BF16)
        take(w, g, B1P, 2 * ROWS)
        s2[j, 0, :ROWS, :] = (pf[g, half(yp, 0), :] + r1[j, 0].astype(F32)).astype(BF16)
        go(w, g, B2P)
        s2[j, 1, ROWS:, :] = (pf[g, half(ym, 1), :] + r1[j, 1].astype(F32)).astype(BF16)
        go(w, g, B2M)

    def b3(w, g):
        j = w * 4 + g // 2
        take(w, g, B2P, 4 * ROWS)

        def total(z):
            rows = rng(z * ROWS, ROWS)
            return pf[g, half(y, z), :] + r2[j, 0, rows, :].astype(F32) + r2[j, 1, rows, :].astype(F32)

        s3[j] = total(1 - zh).astype(BF16)
        go(w, g, B3)
        fin[j] = total(zh)

    def b4(w, g):
        j = w * 4 + g // 2
        take(w, g, B3, ROWS)
        result(w, g, fin[j] + r3[j].astype(F32))

    def w1(w, g):
        j = w * 4 + g // 2
        for s in range(4):
            w0s[j, s] = pf[g, half(s, 1 - zh), :].astype(BF16)
        go(w, g, W0)

    def w2(w, g):
        j = w * 4 + g // 2
        take(w, g, W0, 4 * ROWS)
        for s in range(4):
            pf[g, half(s, zh), :] += w0r[j, s].astype(F32)
        w1s[j, 0] = pf[g, quarter(yo, zh, 0), :].astype(BF16)
        w1s[j, 1] = pf[g, quarter(yo, zh, 1), :].astype(BF16)
        go(w, g, W1P, W1M)

    def w3(w, g):
        j = w * 4 + g // 2
        w2s[j, 0, 64:, :] = pf[g, quarter(yp, zh, 1), :].astype(BF16)
        w2s[j, 1, :64, :] = pf[g, quarter(ym, zh, 0), :].astype(BF16)
        take(w, g, W1P, ROWS)
        w2s[j, 0, :64, :] = (pf[g, quarter(yp, zh, 0), :] + w1r[j, 0].astype(F32)).astype(BF16)
        go(w, g, W2P)
        w2s[j, 1, 64:, :] = (pf[g, quarter(ym, zh, 1), :] + w1r[j, 1].astype(F32)).astype(BF16)
        go(w, g, W2M)

    def w4(w, g):
        j = w * 4 + g // 2
        take(w, g, W2P, 2 * ROWS)
        result(w, g, pf[g, own, :] + w2r[j, 0].astype(F32) + w2r[j, 1].astype(F32))

    def result(w, g, total):
        total = total.astype(BF16)
        if w:
            dk_ref[0, :, rng(g * HD, HD)] = total
        else:
            dv_ref[0, :, rng(g * HD, HD)] = total
            vgb[g // 2, rng(me * ROWS, ROWS), rng(lax.rem(g, 2) * HD, HD)] = total

    dv = [None] + [either(0, *two) for two in ((b1, w1), (b2, w2), (b3, w3), (b4, w4))]
    dk = [None] + [either(1, *two) for two in ((b1, w1), (b2, w2), (b3, w3), (b4, w4))]

    def send_h(k, z):
        xx, cc, to = near(k)
        return pltpu.make_async_remote_copy(
            src_ref=ht.at[rng(((xx * 2 + z) * 2 + cc) * 320, 320)],
            dst_ref=hg.at[z, :, rng(me * ROWS, ROWS)],
            send_sem=hs.at[0], recv_sem=hr.at[0], device_id=to, device_id_type=MESH,
        )

    def turn(i):
        dx, z = i // 2, lax.rem(i, 2)
        j = lax.rem(x + dx, 4) * 2 + z
        for n in range(5):
            at = j * 640 + n * 128
            ht[rng(at, 128), :] = hid[:, rng(at, 128)].T
        send_h(dx * 2 + 1, z).start()

        @pl.when(dx > 0)
        def _():
            send_h(dx * 2, z).start()

        @pl.when(dx == 0)
        def _():
            hg[z, :, rng(me * ROWS, ROWS)] = ht[rng((j * 2 + core) * 320, 320), :]

    def send_v(k, p):
        rows = rng(me * ROWS, ROWS)
        return pltpu.make_async_remote_copy(
            src_ref=vgb.at[p, rows], dst_ref=vgb.at[p, rows], send_sem=vs.at[0], recv_sem=vr.at[p],
            device_id=near(k)[2], device_id_type=MESH,
        )

    def send_w(k, p):
        yy, to = along_y(k)
        return pltpu.make_async_remote_copy(
            src_ref=dws.at[p, yy], dst_ref=dwr.at[p, k], send_sem=ws.at[0], recv_sem=wr.at[p],
            device_id=to, device_id_type=MESH,
        )

    def send_u(k, p):
        t, to = along_z(k)
        return pltpu.make_async_remote_copy(
            src_ref=dus.at[p, t], dst_ref=dur.at[p, k], send_sem=us.at[0], recv_sem=ur.at[p],
            device_id=to, device_id_type=MESH,
        )

    def weights1(p):
        each(1, 8, lambda k: send_v(k, p).start())

    def weights2(p):
        @pl.when(p == 0)
        def _():
            wait(hg.at[:, :, pl.ds(0, 7 * ROWS)], hr.at[0])

        wait(vgb.at[p, pl.ds(0, 7 * ROWS)], vr.at[p])
        res = dot(hg[...].reshape(640, SEQ), vgb[p], 1, 0).reshape(16, 40, 256)
        res = jnp.concatenate([res[:, :, :128], res[:, :, 128:]], axis=1).astype(BF16)
        for t in range(16):
            dws[p, (t // 2) % 4, t // 8 * 2 + t % 2] = res[t]
        each(1, 4, lambda k: send_w(k, p).start())

    def weights3(p):
        wait(dwr.at[p, pl.ds(0, 3)], wr.at[p])
        acc = dws[p, y].astype(F32)
        for k in range(1, 4):
            acc = acc + dwr[p, k].astype(F32)
        dus[p] = acc.astype(BF16)
        each(1, 4, lambda k: send_u(k, p).start())

    def weights4(p):
        wait(dur.at[p, pl.ds(0, 3)], ur.at[p])
        acc = dus[p, mine].astype(F32)
        for k in range(1, 4):
            acc = acc + dur[p, k].astype(F32)
        dw_ref[:, rng(p * 256, 128)] = acc[:40]
        dw_ref[:, rng(p * 256 + 128, 128)] = acc[40:]

    def at(i, lo, count, f):
        @pl.when((i >= lo) & (i < lo + count))
        def _():
            f(i - lo)

    def at_pair(i, lo, f):
        @pl.when((i >= lo) & (i < lo + 8) & (lax.rem(i - lo, 2) == 0))
        def _():
            f((i - lo) // 2)

    def step(i, c):
        at(i, K1, KVH, keys[1])
        at(i, K2, KVH, keys[2])
        at(i, V0, KVH, values[0])
        at(i, V1, KVH, values[1])
        at(i, V2, KVH, values[2])

        @pl.when(i < KVH)
        def _():
            rows_of(i)
            keys[3](i)
            pass1(i)
            dv[1](i)

        at(i, D2, KVH, dv[2])
        at(i, D3, KVH, dv[3])
        at(i, D4, KVH, dv[4])
        at_pair(i, G1, weights1)

        @pl.when(i < 4)
        def _():
            turn(2 * i)
            turn(2 * i + 1)

        @pl.when((i >= KVH) & (i < 2 * KVH))
        def _():
            g = i - KVH
            values[3](g)
            pass2(g)
            dk[1](g)

        at(i, E2, KVH, dk[2])
        at(i, E3, KVH, dk[3])
        at(i, E4, KVH, dk[4])
        at_pair(i, G2, weights2)
        at_pair(i, G3, weights3)
        at_pair(i, G4, weights4)
        return c

    lax.fori_loop(0, E4 + KVH, step, 0)

    every = kvb.at[:, 0, pl.ds(0, SENT)]
    for w in range(2):
        for n in range(2):
            wait(every, send.at[w, n])
    wait(ob, dqsem.at[0])
    wait(hg.at[:, :, pl.ds(0, 7 * ROWS)], hs.at[0])
    wait(vgb.at[:, pl.ds(0, 7 * ROWS)], vs.at[0])
    wait(dws.at[:, pl.ds(0, 3)], ws.at[0])
    wait(dus.at[:, pl.ds(0, 3)], us.at[0])


def copy_out(dq, dk, dv, dw, dq_out, dk_out, dv_out, dw_out, dq_v, dk_v, dv_v, dw_v, into, out):
    parts = [(dk, dk_v, dk_out), (dv, dv_v, dv_out), (dw, dw_v, dw_out)]
    for n in range(8):
        cols = pl.ds(n * 1024, 1024)
        parts.append((dq.at[:, :, cols], dq_v.at[n], dq_out.at[:, :, cols]))
    reads = [pltpu.make_async_copy(a, b, into.at[n]) for n, (a, b, _) in enumerate(parts)]
    writes = [pltpu.make_async_copy(b, c, out.at[n]) for n, (_, b, c) in enumerate(parts)]
    for copy in reads:
        copy.start()
    for read, write in zip(reads, writes):
        read.wait()
        write.start()
    for copy in writes:
        copy.wait()


def body(hidden, q, k, v, o, do, lse, docs, order):
    anyspace = pl.BlockSpec(memory_space=pl.ANY)
    vmem = pl.BlockSpec(memory_space=pltpu.VMEM)
    smem = pl.BlockSpec(memory_space=pltpu.SMEM)
    dma = pltpu.SemaphoreType.DMA
    shapes = (
        jax.ShapeDtypeStruct((1, ROWS, KVH * GRP * HD), BF16),
        jax.ShapeDtypeStruct((1, ROWS, KVH * HD), BF16),
        jax.ShapeDtypeStruct((1, ROWS, KVH * HD), BF16),
        jax.ShapeDtypeStruct((40, KVH * HD), F32),
    )
    results = pl.pallas_call(
        kernel,
        out_shape=shapes,
        in_specs=[smem, smem] + [anyspace] * 7,
        out_specs=(anyspace, vmem, vmem, vmem),
        scratch_shapes=[
            pltpu.VMEM((KVH, 2, SEQ, HD), BF16),
            pltpu.VMEM((KVH, ROWS, GRP * HD), BF16),
            pltpu.VMEM((KVH, ROWS, GRP * HD), BF16),
            pltpu.VMEM((KVH, ROWS, GRP * HD), BF16),
            pltpu.VMEM((SEQ, ROWS), F32),
            pltpu.VMEM((KVH, 1, GRP * ROWS), F32),
            pltpu.VMEM((KVH, 1, GRP * ROWS), F32),
            pltpu.VMEM((KVH, SEQ, HD), F32),
            pltpu.VMEM((HD, GRP * ROWS), F32),
            pltpu.VMEM((KVH, SEQ, GRP * ROWS), BF16),
            pltpu.VMEM((KVH * GRP, ROWS), F32),
            pltpu.VMEM((KVH, 2, ROWS, HD), BF16),
            pltpu.VMEM((KVH, 2, ROWS, HD), BF16),
            pltpu.VMEM((KVH, 2, 2 * ROWS, HD), BF16),
            pltpu.VMEM((KVH, 2, 2 * ROWS, HD), BF16),
            pltpu.VMEM((KVH, ROWS, HD), BF16),
            pltpu.VMEM((KVH, ROWS, HD), BF16),
            pltpu.VMEM((KVH, ROWS, HD), F32),
            pltpu.VMEM((KVH, 4, ROWS, HD), BF16),
            pltpu.VMEM((KVH, 4, ROWS, HD), BF16),
            pltpu.VMEM((KVH, 2, 64, HD), BF16),
            pltpu.VMEM((KVH, 2, 64, HD), BF16),
            pltpu.VMEM((KVH, 2, ROWS, HD), BF16),
            pltpu.VMEM((KVH, 2, ROWS, HD), BF16),
            pltpu.VMEM((ROWS, 5120), BF16),
            pltpu.VMEM((5120, ROWS), BF16),
            pltpu.VMEM((2, 320, SEQ), BF16),
            pltpu.VMEM((4, SEQ, 256), BF16),
            pltpu.VMEM((4, 4, 4, 80, 128), BF16),
            pltpu.VMEM((4, 4, 4, 80, 128), BF16),
            pltpu.VMEM((4, 4, 80, 128), BF16),
            pltpu.VMEM((4, 4, 80, 128), BF16),
            dma((2, 2)), dma((6, 2 * KVH)), dma((3,)), dma((KVH,)), dma((1,)),
            dma((1,)), dma((1,)), dma((1,)), dma((4,)), dma((1,)), dma((4,)), dma((1,)), dma((4,)),
        ],
        compiler_params=pltpu.CompilerParams(
            collective_id=0, has_side_effects=True, vmem_limit_bytes=62 * 2**20
        ),
        name="attention_and_weights",
    )(docs, order, q, k, v, o, do, lse, hidden)
    return pl.pallas_call(
        copy_out,
        out_shape=shapes,
        in_specs=[anyspace] * 4,
        out_specs=(anyspace,) * 4,
        scratch_shapes=[
            pltpu.VMEM((8, 1, ROWS, 1024), BF16),
            pltpu.VMEM((1, ROWS, KVH * HD), BF16),
            pltpu.VMEM((1, ROWS, KVH * HD), BF16),
            pltpu.VMEM((40, KVH * HD), F32),
            dma((11,)), dma((11,)),
        ],
        name="copy_out",
    )(*results)


def solution(mesh):
    placed = (P("dp", "ctx", None),) * 6 + (P("dp", None, "ctx"), P("dp", None), P("dp", None))
    return jax.shard_map(
        body,
        mesh=mesh,
        in_specs=placed,
        out_specs=(P("dp", "ctx", None),) * 3 + (P(("dp", "ctx"), None),),
        check_vma=False,
    )
```

time: 118 us -> 94.4 us (0.80)
  Pallas kernels: 112 us -> 93.5 us
  local copies, waits for them, and re-layouts: 5.24 us -> 0 us
    pallas_call x1 -> x2, Pallas kernels: 112 us -> 93.5 us  [the longest x1 90.8 us: body(): pl.pallas_call(kernel, out_shape=shapes, in_specs=[smem, smem] + [anyspac...]
    unnamed x10 -> x0, local copies, waits for them, and re-layouts: 5.24 us -> none
where the time goes in v3:
time: 94.4 us; the launch traced here: 94.1 us
  Pallas kernels  93.5 us (99%)
    pallas_call x1, Pallas kernels, body(): pl.pallas_call(kernel, out_shape=shapes, in_specs=[smem, smem] + [anyspac...  90.8 us
    pallas_call x1, Pallas kernels, body(): pl.pallas_call(copy_out, out_shape=shapes, in_specs=[anyspace] * 4, out_s...  2.67 us

profile of v3, /device:TPU:0, one launch (start us, length us, event | category | flops | bytes accessed | tf_op | source)
XLA Modules:
  0.0 94.1 jit_solution(7887209088069134859)
XLA Ops:
  0.6 90.8 %attention_and_weights.1 = (bf16[1,128,8192]{2,1,0:T(8,128)(2,1)}, bf16[1,128,1024]{2,1,0:T(8,128)(2,1)}, bf16[1,128,1024]{2,1,0:T(8,128)(2,1)}, f32[40,1024]{1,0:T(8,128)}) custom-call(s32[1,8]{1,0:T(1,128)} %doc_ref.1, s32[1,16]{1,0:T(1,128)} %ord_ref.1, bf16[1,128,8192]{2,1,0:T(8,128)(2,1)} %q_ref.1, bf16[1,128,1024]{2,1,0:T(8,128)(2,1)} %k_ref.1, ...), custom_call_target="tpu_custom_call" | custom-call | tf_op jit(solution)/shard_map/attention_and_weights/pallas_call | solution.py:529
  91.5 2.7 %copy_out.1 = (bf16[1,128,8192]{2,1,0:T(8,128)(2,1)}, bf16[1,128,1024]{2,1,0:T(8,128)(2,1)}, bf16[1,128,1024]{2,1,0:T(8,128)(2,1)}, f32[40,1024]{1,0:T(8,128)}) custom-call(bf16[1,128,8192]{2,1,0:T(8,128)(2,1)} %get-tuple-element.8.dq, bf16[1,128,1024]{2,1,0:T(8,128)(2,1)} %get-tuple-element.9.dk, bf16[1,128,1024]{2,1,0:T(8,128)(2,1)} %get-tuple-element.10.dv, ...), custom_call_target="tpu_custom_call" | custom-call | tf_op jit(solution)/shard_map/copy_out/pallas_call | solution.py:575

commit v4 on v3

--- a/solution.py
+++ b/solution.py
@@ -19,10 +19,12 @@
 LOG2E = math.log2(math.e)
 BIG = 3.0e38
 NB = 1024
-K1, K2, V0, V1, V2 = -6, -3, 0, 3, 6
-D2, D3, D4 = 3, 6, 8
-E2, E3, E4 = 11, 14, 17
-G1, G2, G3, G4 = 9, 12, 14, 16
+K1, K2, V0, V1, V2 = (-8, 1), (-4, 1), (0, 1), (3, 1), (6, 1)
+P1, P2 = (0, 1), (8, 1)
+D2, D3, D4 = (3, 1), (6, 1), (8, 1)
+E2, E3, E4 = (11, 1), (14, 1), (17, 1)
+G1, GB, G2, G3, G4 = (9, 2), (10, 2), (11, 2), (13, 2), (15, 2)
+TICKS = 25
 
 A0, A1P, A1M, A3P, A3M = range(5)
 V1P, V1M, V2P, V2M, Z0, ZP, ZM, ZO = range(5, 13)
@@ -43,10 +45,10 @@
 def kernel(
     doc_ref, ord_ref, q_ref, k_ref, v_ref, o_ref, do_ref, lse_ref, h_ref,
     dq_ref, dk_ref, dv_ref, dw_ref,
-    kvb, qb, dob, ob, cap, lser, deltar, pf, dqt, probs, lse,
+    kvb, qb, dob, ob, cap, lser, deltar, pf, dqt, lse,
     s1, r1, s2, r2, s3, r3, fin, w0s, w0r, w1s, w1r, w2s, w2r,
     hid, ht, hg, vgb, dws, dwr, dus, dur,
-    send, recv, lsem, hsem, dqsem, hs, hr, vs, vr, ws, wr, us, ur,
+    send, recv, lsem, hsem, dqsem, hs, hr, vs, vr, vc, ws, wr, us, ur,
 ):
     dp, ctx = lax.axis_index("dp"), lax.axis_index("ctx")
     x, zl, core = dp // 4, lax.rem(dp // 2, 2), lax.rem(dp, 2)
@@ -112,7 +114,7 @@
             ZM: (half(ym, zh), partner),
             ZO: (half(yo, zh), partner),
         }
-        j = w * 4 + g // 2
+        j = w * KVH + g
         other = {
             B1P: (s1.at[j, 0], r1.at[j, 0], up),
             B1M: (s1.at[j, 1], r1.at[j, 1], down),
@@ -155,13 +157,13 @@
 
     def either(w, first, second):
         def run(g):
-            even = lax.rem(g + w, 2) == 0
-
-            @pl.when(even)
+            most = lax.rem(g * 5 + w * 4, 8) < 5
+
+            @pl.when(most)
             def _():
                 first(w, g)
 
-            @pl.when(jnp.logical_not(even))
+            @pl.when(jnp.logical_not(most))
             def _():
                 second(w, g)
 
@@ -233,13 +235,11 @@
         seen = (pos_n <= pos_q) & (pos_n >= start_q)
         cap[j * 64:(j + 1) * 64, :] = jnp.where(seen, BIG, -BIG)
 
-    each(0, -K1, keys[1])
-    each(0, -V0, values[0])
+    each(0, -K1[0], keys[1])
+    each(0, -min(V0[0], 0), values[0])
     load_hidden.wait()
     load_lse.wait()
-    each(0, -K2, keys[2])
-    each(0, -V1, values[1])
-    each(0, -V2, values[2])
+    each(0, -K2[0], keys[2])
 
     def rows_of(g):
         wait(kvb.at[pl.ds(0, 3), 0], hsem.at[g])
@@ -253,16 +253,18 @@
     def stack(ref, g):
         return jnp.concatenate([ref[g, :, h * HD:(h + 1) * HD] for h in range(GRP)], axis=0)
 
+    def probs(g, r, qq):
+        top = jnp.concatenate([cap[r, :]] * GRP, axis=1)
+        st = dot(kvb[g, 0, r, :], qq, 1, 1)
+        return jnp.exp2(jnp.minimum(st * (SCALE * LOG2E) - lser[g], top))
+
     def pass1(g):
         qq, dd = stack(qb, g), stack(dob, g)
 
         def block(nb, c):
             r = rng(nb * NB, NB)
-            top = jnp.concatenate([cap[r, :]] * GRP, axis=1)
-            st = dot(kvb[g, 0, r, :], qq, 1, 1)
-            p = jnp.exp2(jnp.minimum(st * (SCALE * LOG2E) - lser[g], top)).astype(BF16)
-            probs[g, r, :] = p
-            pf[g, r, :] = dot(p, dd, 1, 0)
+            p = probs(g, r, qq).astype(BF16)
+            pf[0, g, r, :] = dot(p, dd, 1, 0)
             return c
 
         lax.fori_loop(0, SEQ // NB, block, 0)
@@ -272,9 +274,10 @@
 
         def block(nb):
             r = rng(nb * NB, NB)
+            p = probs(g, r, qq)
             dp_ = dot(kvb[g, 1, r, :], dd, 1, 1)
-            ds = (probs[g, r, :].astype(F32) * (dp_ * SCALE - deltar[g])).astype(BF16)
-            pf[g, r, :] = dot(ds, qq, 1, 0)
+            ds = (p * (dp_ * SCALE - deltar[g])).astype(BF16)
+            pf[1, g, r, :] = dot(ds, qq, 1, 0)
             dqt[...] = (dqt[...] if nb else 0.0) + dot(kvb[g, 0, r, :].T, ds, 1, 0)
 
         for nb in range(SEQ // NB):
@@ -288,67 +291,67 @@
         return pltpu.make_async_copy(ob.at[g], dq_ref.at[0, :, rng(g * GRP * HD, GRP * HD)], dqsem.at[0])
 
     def b1(w, g):
-        j = w * 4 + g // 2
-        s1[j, 0] = pf[g, half(yo, 0), :].astype(BF16)
-        s1[j, 1] = pf[g, half(yo, 1), :].astype(BF16)
+        j = w * KVH + g
+        s1[j, 0] = pf[w, g, half(yo, 0), :].astype(BF16)
+        s1[j, 1] = pf[w, g, half(yo, 1), :].astype(BF16)
         go(w, g, B1P, B1M)
 
     def b2(w, g):
-        j = w * 4 + g // 2
-        s2[j, 0, ROWS:, :] = pf[g, half(yp, 1), :].astype(BF16)
-        s2[j, 1, :ROWS, :] = pf[g, half(ym, 0), :].astype(BF16)
+        j = w * KVH + g
+        s2[j, 0, ROWS:, :] = pf[w, g, half(yp, 1), :].astype(BF16)
+        s2[j, 1, :ROWS, :] = pf[w, g, half(ym, 0), :].astype(BF16)
         take(w, g, B1P, 2 * ROWS)
-        s2[j, 0, :ROWS, :] = (pf[g, half(yp, 0), :] + r1[j, 0].astype(F32)).astype(BF16)
+        s2[j, 0, :ROWS, :] = (pf[w, g, half(yp, 0), :] + r1[j, 0].astype(F32)).astype(BF16)
         go(w, g, B2P)
-        s2[j, 1, ROWS:, :] = (pf[g, half(ym, 1), :] + r1[j, 1].astype(F32)).astype(BF16)
+        s2[j, 1, ROWS:, :] = (pf[w, g, half(ym, 1), :] + r1[j, 1].astype(F32)).astype(BF16)
         go(w, g, B2M)
 
     def b3(w, g):
-        j = w * 4 + g // 2
+        j = w * KVH + g
         take(w, g, B2P, 4 * ROWS)
 
         def total(z):
             rows = rng(z * ROWS, ROWS)
-            return pf[g, half(y, z), :] + r2[j, 0, rows, :].astype(F32) + r2[j, 1, rows, :].astype(F32)
+            return pf[w, g, half(y, z), :] + r2[j, 0, rows, :].astype(F32) + r2[j, 1, rows, :].astype(F32)
 
         s3[j] = total(1 - zh).astype(BF16)
         go(w, g, B3)
         fin[j] = total(zh)
 
     def b4(w, g):
-        j = w * 4 + g // 2
+        j = w * KVH + g
         take(w, g, B3, ROWS)
         result(w, g, fin[j] + r3[j].astype(F32))
 
     def w1(w, g):
-        j = w * 4 + g // 2
+        j = w * KVH + g
         for s in range(4):
-            w0s[j, s] = pf[g, half(s, 1 - zh), :].astype(BF16)
+            w0s[j, s] = pf[w, g, half(s, 1 - zh), :].astype(BF16)
         go(w, g, W0)
 
     def w2(w, g):
-        j = w * 4 + g // 2
+        j = w * KVH + g
         take(w, g, W0, 4 * ROWS)
         for s in range(4):
-            pf[g, half(s, zh), :] += w0r[j, s].astype(F32)
-        w1s[j, 0] = pf[g, quarter(yo, zh, 0), :].astype(BF16)
-        w1s[j, 1] = pf[g, quarter(yo, zh, 1), :].astype(BF16)
+            pf[w, g, half(s, zh), :] += w0r[j, s].astype(F32)
+        w1s[j, 0] = pf[w, g, quarter(yo, zh, 0), :].astype(BF16)
+        w1s[j, 1] = pf[w, g, quarter(yo, zh, 1), :].astype(BF16)
         go(w, g, W1P, W1M)
 
     def w3(w, g):
-        j = w * 4 + g // 2
-        w2s[j, 0, 64:, :] = pf[g, quarter(yp, zh, 1), :].astype(BF16)
-        w2s[j, 1, :64, :] = pf[g, quarter(ym, zh, 0), :].astype(BF16)
+        j = w * KVH + g
+        w2s[j, 0, 64:, :] = pf[w, g, quarter(yp, zh, 1), :].astype(BF16)
+        w2s[j, 1, :64, :] = pf[w, g, quarter(ym, zh, 0), :].astype(BF16)
         take(w, g, W1P, ROWS)
-        w2s[j, 0, :64, :] = (pf[g, quarter(yp, zh, 0), :] + w1r[j, 0].astype(F32)).astype(BF16)
+        w2s[j, 0, :64, :] = (pf[w, g, quarter(yp, zh, 0), :] + w1r[j, 0].astype(F32)).astype(BF16)
         go(w, g, W2P)
-        w2s[j, 1, 64:, :] = (pf[g, quarter(ym, zh, 1), :] + w1r[j, 1].astype(F32)).astype(BF16)
+        w2s[j, 1, 64:, :] = (pf[w, g, quarter(ym, zh, 1), :] + w1r[j, 1].astype(F32)).astype(BF16)
         go(w, g, W2M)
 
     def w4(w, g):
-        j = w * 4 + g // 2
+        j = w * KVH + g
         take(w, g, W2P, 2 * ROWS)
-        result(w, g, pf[g, own, :] + w2r[j, 0].astype(F32) + w2r[j, 1].astype(F32))
+        result(w, g, pf[w, g, own, :] + w2r[j, 0].astype(F32) + w2r[j, 1].astype(F32))
 
     def result(w, g, total):
         total = total.astype(BF16)
@@ -385,45 +388,50 @@
         def _():
             hg[z, :, rng(me * ROWS, ROWS)] = ht[rng((j * 2 + core) * 320, 320), :]
 
-    def send_v(k, p):
-        rows = rng(me * ROWS, ROWS)
+    def send_v(k, p, n, sem):
+        rows = rng((lax.rem(x + n, 4) * 2 + core) * ROWS, ROWS)
         return pltpu.make_async_remote_copy(
-            src_ref=vgb.at[p, rows], dst_ref=vgb.at[p, rows], send_sem=vs.at[0], recv_sem=vr.at[p],
+            src_ref=vgb.at[p, rows], dst_ref=vgb.at[p, rows], send_sem=vs.at[0], recv_sem=sem.at[p],
             device_id=near(k)[2], device_id_type=MESH,
         )
 
     def send_w(k, p):
+        t, to = along_z(k)
+        return pltpu.make_async_remote_copy(
+            src_ref=dws.at[p, t], dst_ref=dwr.at[p, k], send_sem=ws.at[0], recv_sem=wr.at[p],
+            device_id=to, device_id_type=MESH,
+        )
+
+    def send_u(k, p):
         yy, to = along_y(k)
         return pltpu.make_async_remote_copy(
-            src_ref=dws.at[p, yy], dst_ref=dwr.at[p, k], send_sem=ws.at[0], recv_sem=wr.at[p],
+            src_ref=dus.at[p, yy], dst_ref=dur.at[p, k], send_sem=us.at[0], recv_sem=ur.at[p],
             device_id=to, device_id_type=MESH,
         )
 
-    def send_u(k, p):
-        t, to = along_z(k)
-        return pltpu.make_async_remote_copy(
-            src_ref=dus.at[p, t], dst_ref=dur.at[p, k], send_sem=us.at[0], recv_sem=ur.at[p],
-            device_id=to, device_id_type=MESH,
-        )
-
     def weights1(p):
-        each(1, 8, lambda k: send_v(k, p).start())
+        each(1, 4, lambda n: send_v(2 * n, p, 0, vr).start())
+        send_v(1, p, 0, vc).start()
+
+    def weights1b(p):
+        wait(vgb.at[p, pl.ds(0, 3 * ROWS)], vr.at[p])
+        each(1, 4, lambda n: send_v(1, p, n, vc).start())
 
     def weights2(p):
         @pl.when(p == 0)
         def _():
             wait(hg.at[:, :, pl.ds(0, 7 * ROWS)], hr.at[0])
 
-        wait(vgb.at[p, pl.ds(0, 7 * ROWS)], vr.at[p])
+        wait(vgb.at[p, pl.ds(0, 4 * ROWS)], vc.at[p])
         res = dot(hg[...].reshape(640, SEQ), vgb[p], 1, 0).reshape(16, 40, 256)
         res = jnp.concatenate([res[:, :, :128], res[:, :, 128:]], axis=1).astype(BF16)
         for t in range(16):
-            dws[p, (t // 2) % 4, t // 8 * 2 + t % 2] = res[t]
+            dws[p, t // 8 * 2 + t % 2, (t // 2) % 4] = res[t]
         each(1, 4, lambda k: send_w(k, p).start())
 
     def weights3(p):
         wait(dwr.at[p, pl.ds(0, 3)], wr.at[p])
-        acc = dws[p, y].astype(F32)
+        acc = dws[p, mine].astype(F32)
         for k in range(1, 4):
             acc = acc + dwr[p, k].astype(F32)
         dus[p] = acc.astype(BF16)
@@ -431,62 +439,54 @@
 
     def weights4(p):
         wait(dur.at[p, pl.ds(0, 3)], ur.at[p])
-        acc = dus[p, mine].astype(F32)
+        acc = dus[p, y].astype(F32)
         for k in range(1, 4):
             acc = acc + dur[p, k].astype(F32)
         dw_ref[:, rng(p * 256, 128)] = acc[:40]
         dw_ref[:, rng(p * 256 + 128, 128)] = acc[40:]
 
-    def at(i, lo, count, f):
-        @pl.when((i >= lo) & (i < lo + count))
+    def at(i, when, count, f):
+        lo, stride = when
+        n = i - lo
+
+        @pl.when((n >= 0) & (n < count * stride) & (lax.rem(n, stride) == 0))
         def _():
-            f(i - lo)
-
-    def at_pair(i, lo, f):
-        @pl.when((i >= lo) & (i < lo + 8) & (lax.rem(i - lo, 2) == 0))
-        def _():
-            f((i - lo) // 2)
+            f(n // stride)
+
+    def first(g):
+        rows_of(g)
+        keys[3](g)
+        pass1(g)
+        dv[1](g)
+
+    def second(g):
+        values[3](g)
+        pass2(g)
+        dk[1](g)
 
     def step(i, c):
+        at(i, E4, KVH, dk[4])
+        at(i, E3, KVH, dk[3])
+        at(i, E2, KVH, dk[2])
+        at(i, D4, KVH, dv[4])
+        at(i, G1, 4, weights1)
+        at(i, GB, 4, weights1b)
+        at(i, G2, 4, weights2)
+        at(i, G3, 4, weights3)
+        at(i, G4, 4, weights4)
+        at(i, D3, KVH, dv[3])
+        at(i, D2, KVH, dv[2])
         at(i, K1, KVH, keys[1])
         at(i, K2, KVH, keys[2])
         at(i, V0, KVH, values[0])
         at(i, V1, KVH, values[1])
         at(i, V2, KVH, values[2])
-
-        @pl.when(i < KVH)
-        def _():
-            rows_of(i)
-            keys[3](i)
-            pass1(i)
-            dv[1](i)
-
-        at(i, D2, KVH, dv[2])
-        at(i, D3, KVH, dv[3])
-        at(i, D4, KVH, dv[4])
-        at_pair(i, G1, weights1)
-
-        @pl.when(i < 4)
-        def _():
-            turn(2 * i)
-            turn(2 * i + 1)
-
-        @pl.when((i >= KVH) & (i < 2 * KVH))
-        def _():
-            g = i - KVH
-            values[3](g)
-            pass2(g)
-            dk[1](g)
-
-        at(i, E2, KVH, dk[2])
-        at(i, E3, KVH, dk[3])
-        at(i, E4, KVH, dk[4])
-        at_pair(i, G2, weights2)
-        at_pair(i, G3, weights3)
-        at_pair(i, G4, weights4)
+        at(i, (0, 1), KVH, turn)
+        at(i, P1, KVH, first)
+        at(i, P2, KVH, second)
         return c
 
-    lax.fori_loop(0, E4 + KVH, step, 0)
+    lax.fori_loop(0, TICKS, step, 0)
 
     every = kvb.at[:, 0, pl.ds(0, SENT)]
     for w in range(2):
@@ -539,23 +539,22 @@
             pltpu.VMEM((SEQ, ROWS), F32),
             pltpu.VMEM((KVH, 1, GRP * ROWS), F32),
             pltpu.VMEM((KVH, 1, GRP * ROWS), F32),
-            pltpu.VMEM((KVH, SEQ, HD), F32),
+            pltpu.VMEM((2, KVH, SEQ, HD), F32),
             pltpu.VMEM((HD, GRP * ROWS), F32),
-            pltpu.VMEM((KVH, SEQ, GRP * ROWS), BF16),
             pltpu.VMEM((KVH * GRP, ROWS), F32),
-            pltpu.VMEM((KVH, 2, ROWS, HD), BF16),
-            pltpu.VMEM((KVH, 2, ROWS, HD), BF16),
-            pltpu.VMEM((KVH, 2, 2 * ROWS, HD), BF16),
-            pltpu.VMEM((KVH, 2, 2 * ROWS, HD), BF16),
-            pltpu.VMEM((KVH, ROWS, HD), BF16),
-            pltpu.VMEM((KVH, ROWS, HD), BF16),
-            pltpu.VMEM((KVH, ROWS, HD), F32),
-            pltpu.VMEM((KVH, 4, ROWS, HD), BF16),
-            pltpu.VMEM((KVH, 4, ROWS, HD), BF16),
-            pltpu.VMEM((KVH, 2, 64, HD), BF16),
-            pltpu.VMEM((KVH, 2, 64, HD), BF16),
-            pltpu.VMEM((KVH, 2, ROWS, HD), BF16),
-            pltpu.VMEM((KVH, 2, ROWS, HD), BF16),
+            pltpu.VMEM((2 * KVH, 2, ROWS, HD), BF16),
+            pltpu.VMEM((2 * KVH, 2, ROWS, HD), BF16),
+            pltpu.VMEM((2 * KVH, 2, 2 * ROWS, HD), BF16),
+            pltpu.VMEM((2 * KVH, 2, 2 * ROWS, HD), BF16),
+            pltpu.VMEM((2 * KVH, ROWS, HD), BF16),
+            pltpu.VMEM((2 * KVH, ROWS, HD), BF16),
+            pltpu.VMEM((2 * KVH, ROWS, HD), F32),
+            pltpu.VMEM((2 * KVH, 4, ROWS, HD), BF16),
+            pltpu.VMEM((2 * KVH, 4, ROWS, HD), BF16),
+            pltpu.VMEM((2 * KVH, 2, 64, HD), BF16),
+            pltpu.VMEM((2 * KVH, 2, 64, HD), BF16),
+            pltpu.VMEM((2 * KVH, 2, ROWS, HD), BF16),
+            pltpu.VMEM((2 * KVH, 2, ROWS, HD), BF16),
             pltpu.VMEM((ROWS, 5120), BF16),
             pltpu.VMEM((5120, ROWS), BF16),
             pltpu.VMEM((2, 320, SEQ), BF16),
@@ -565,7 +564,7 @@
             pltpu.VMEM((4, 4, 80, 128), BF16),
             pltpu.VMEM((4, 4, 80, 128), BF16),
             dma((2, 2)), dma((6, 2 * KVH)), dma((3,)), dma((KVH,)), dma((1,)),
-            dma((1,)), dma((1,)), dma((1,)), dma((4,)), dma((1,)), dma((4,)), dma((1,)), dma((4,)),
+            dma((1,)), dma((1,)), dma((1,)), dma((4,)), dma((4,)), dma((1,)), dma((4,)), dma((1,)), dma((4,)),
         ],
         compiler_params=pltpu.CompilerParams(
             collective_id=0, has_side_effects=True, vmem_limit_bytes=62 * 2**20

time: 94.4 us -> 92.4 us (0.979)
  Pallas kernels: 93.5 us -> 91.1 us
    pallas_call x1, Pallas kernels: 90.8 us -> 88.4 us  [body(): pl.pallas_call(kernel, out_shape=shapes, in_specs=[smem, smem] + [anyspac...]
where the time goes in v4:
time: 92.4 us; the launch traced here: 91.7 us
  Pallas kernels  91.1 us (99%)
    pallas_call x1, Pallas kernels, body(): pl.pallas_call(kernel, out_shape=shapes, in_specs=[smem, smem] + [anyspac...  88.4 us
    pallas_call x1, Pallas kernels, body(): pl.pallas_call(copy_out, out_shape=shapes, in_specs=[anyspace] * 4, out_s...  2.67 us

profile of v4, /device:TPU:0, one launch (start us, length us, event | category | flops | bytes accessed | tf_op | source)
XLA Modules:
  0.0 91.7 jit_solution(18438322754740768150)
XLA Ops:
  0.6 88.4 %attention_and_weights.1 = (bf16[1,128,8192]{2,1,0:T(8,128)(2,1)}, bf16[1,128,1024]{2,1,0:T(8,128)(2,1)}, bf16[1,128,1024]{2,1,0:T(8,128)(2,1)}, f32[40,1024]{1,0:T(8,128)}) custom-call(s32[1,8]{1,0:T(1,128)} %doc_ref.1, s32[1,16]{1,0:T(1,128)} %ord_ref.1, bf16[1,128,8192]{2,1,0:T(8,128)(2,1)} %q_ref.1, bf16[1,128,1024]{2,1,0:T(8,128)(2,1)} %k_ref.1, ...), custom_call_target="tpu_custom_call" | custom-call | tf_op jit(solution)/shard_map/attention_and_weights/pallas_call | solution.py:529
  89.0 2.7 %copy_out.1 = (bf16[1,128,8192]{2,1,0:T(8,128)(2,1)}, bf16[1,128,1024]{2,1,0:T(8,128)(2,1)}, bf16[1,128,1024]{2,1,0:T(8,128)(2,1)}, f32[40,1024]{1,0:T(8,128)}) custom-call(bf16[1,128,8192]{2,1,0:T(8,128)(2,1)} %get-tuple-element.8.dq, bf16[1,128,1024]{2,1,0:T(8,128)(2,1)} %get-tuple-element.9.dk, bf16[1,128,1024]{2,1,0:T(8,128)(2,1)} %get-tuple-element.10.dv, ...), custom_call_target="tpu_custom_call" | custom-call | tf_op jit(solution)/shard_map/copy_out/pallas_call | solution.py:574

commit v5 on v4

--- a/solution.py
+++ b/solution.py
@@ -278,6 +278,8 @@
             dp_ = dot(kvb[g, 1, r, :], dd, 1, 1)
             ds = (p * (dp_ * SCALE - deltar[g])).astype(BF16)
             pf[1, g, r, :] = dot(ds, qq, 1, 0)
+            if nb == SEQ // NB - 1:
+                dk[1](g)
             dqt[...] = (dqt[...] if nb else 0.0) + dot(kvb[g, 0, r, :].T, ds, 1, 0)
 
         for nb in range(SEQ // NB):
@@ -462,7 +464,6 @@
     def second(g):
         values[3](g)
         pass2(g)
-        dk[1](g)
 
     def step(i, c):
         at(i, E4, KVH, dk[4])

time: 92.4 us -> 93.9 us (1.016)
  Pallas kernels: 91.1 us -> 92.6 us
    pallas_call x1, Pallas kernels: 88.4 us -> 89.9 us  [body(): pl.pallas_call(kernel, out_shape=shapes, in_specs=[smem, smem] + [anyspac...]
where the time goes in v5:
time: 93.9 us; the launch traced here: 93.2 us
  Pallas kernels  92.6 us (99%)
    pallas_call x1, Pallas kernels, body(): pl.pallas_call(kernel, out_shape=shapes, in_specs=[smem, smem] + [anyspac...  89.9 us
    pallas_call x1, Pallas kernels, body(): pl.pallas_call(copy_out, out_shape=shapes, in_specs=[anyspace] * 4, out_s...  2.67 us

profile of v5, /device:TPU:0, one launch (start us, length us, event | category | flops | bytes accessed | tf_op | source)
XLA Modules:
  0.0 93.2 jit_solution(13081905778505449529)
XLA Ops:
  0.6 89.9 %attention_and_weights.1 = (bf16[1,128,8192]{2,1,0:T(8,128)(2,1)}, bf16[1,128,1024]{2,1,0:T(8,128)(2,1)}, bf16[1,128,1024]{2,1,0:T(8,128)(2,1)}, f32[40,1024]{1,0:T(8,128)}) custom-call(s32[1,8]{1,0:T(1,128)} %doc_ref.1, s32[1,16]{1,0:T(1,128)} %ord_ref.1, bf16[1,128,8192]{2,1,0:T(8,128)(2,1)} %q_ref.1, bf16[1,128,1024]{2,1,0:T(8,128)(2,1)} %k_ref.1, ...), custom_call_target="tpu_custom_call" | custom-call | tf_op jit(solution)/shard_map/attention_and_weights/pallas_call | solution.py:530
  90.5 2.7 %copy_out.1 = (bf16[1,128,8192]{2,1,0:T(8,128)(2,1)}, bf16[1,128,1024]{2,1,0:T(8,128)(2,1)}, bf16[1,128,1024]{2,1,0:T(8,128)(2,1)}, f32[40,1024]{1,0:T(8,128)}) custom-call(bf16[1,128,8192]{2,1,0:T(8,128)(2,1)} %get-tuple-element.8.dq, bf16[1,128,1024]{2,1,0:T(8,128)(2,1)} %get-tuple-element.9.dk, bf16[1,128,1024]{2,1,0:T(8,128)(2,1)} %get-tuple-element.10.dv, ...), custom_call_target="tpu_custom_call" | custom-call | tf_op jit(solution)/shard_map/copy_out/pallas_call | solution.py:575
